TPU v7x, 32 devices: a whole 2x2x4 slice. The times are simulated.
32 devices in a mesh: seq: 8 (over z, x), head: 4 (over y, core).
Axes of the slice: x: 2, y: 2, z: 4, core: 2. Of those that a mesh axis runs over, the one named last changes fastest.
Arguments:
- inputs: bfloat16 [4096, 1024], P('seq', 'head'), may hold values from -6 to 6
- lengths: int32 [8], replicated, may hold values from 1 to 4089, as said below
- norm1_gain: bfloat16 [1024], P(('head', 'seq')), may hold values from 0.5 to 1.5
- w_in: bfloat16 [1024, 6144], P('seq', 'head'), may hold values from -0.1875 to 0.1875
- w_small: bfloat16 [1024, 24], P('seq', 'head'), may hold values from -0.375 to 0.375
- conv_weight: bfloat16 [4, 5120], P(None, ('head', 'seq')), may hold values from -3 to 3
- decay_rate: float32 [8], P('head'), as said below
- out_gain: bfloat16 [1024], P(('head', 'seq')), may hold values from 0.5 to 1.5
- w_out: bfloat16 [1024, 1024], P('head', 'seq'), may hold values from -0.375 to 0.375
- norm2_gain: bfloat16 [1024], P(('head', 'seq')), may hold values from 0.5 to 1.5
- w_gate: bfloat16 [1024, 2816], P('seq', 'head'), may hold values from -0.1875 to 0.1875
- w_up: bfloat16 [1024, 2816], P('seq', 'head'), may hold values from -0.1875 to 0.1875
- w_down: bfloat16 [2816, 1024], P('head', 'seq'), may hold values from -0.21875 to 0.21875
- cotangent: bfloat16 [4096, 1024], P('seq', 'head'), may hold values from -6 to 6
Outputs:
- output: bfloat16 [4096, 1024], P('seq', 'head')
- grad_inputs: float32 [4096, 1024], P('seq', 'head')
- grad_norm1_gain: float32 [1024], P(('head', 'seq'))
- grad_w_in: float32 [1024, 6144], P('seq', 'head')
- grad_w_small: float32 [1024, 24], P('seq', 'head')
- grad_conv_weight: float32 [4, 5120], P(None, ('head', 'seq'))
- grad_decay_rate: float32 [8], P('head')
- grad_out_gain: float32 [1024], P(('head', 'seq'))
- grad_w_out: float32 [1024, 1024], P('head', 'seq')
- grad_norm2_gain: float32 [1024], P(('head', 'seq'))
- grad_w_gate: float32 [1024, 2816], P('seq', 'head')
- grad_w_up: float32 [1024, 2816], P('seq', 'head')
- grad_w_down: float32 [2816, 1024], P('head', 'seq')
Inputs may be any that keep to these rules, and one draw needn't show every extreme that they name: 8 document lengths in token order summing to 4096; one document starts within the first 512 tokens and ends within the last 512; every other one has at most 64 tokens. `decay_rate`: one rate a head, between 0.5 / 4096 and 0.05.
All inputs are finite; a program needn't handle non-finite values.
Results may differ from a plain program's by a relative error of at most 0.02125.
Values may be sent and summed in bfloat16 or wider, within the bound.
A program may use at most 192 MiB of HBM per device.

v0:
```python
from functools import partial

import jax
import jax.numpy as jnp
from jax import lax
from jax.sharding import PartitionSpec as P

HOUSE = 2
GROUP = 64


EPSILON = 1e-06
FULL_PRECISION = lax.Precision.HIGHEST


def passed_along(value, axis, steps):
    count = lax.axis_size(axis)
    initial, last = (max(0, -steps), min(count, count - steps))
    return lax.ppermute(value, axis, [(source, source + steps) for source in range(initial, last)])


def document_of(positions, lengths):
    bounds = jnp.cumsum(lengths)
    return jnp.sum((bounds[None, :] <= positions[:, None]).astype(jnp.int32), axis=1)


def unit_rows(values):
    return values * lax.rsqrt(jnp.sum(values * values, axis=-1, keepdims=True) + EPSILON)


def short_conv(extended, owners, kernel):
    count = extended.shape[0] - 3
    current = owners[3:]
    total = kernel[0] * extended[3:]
    for offset in range(1, 4):
        earlier = lax.slice_in_dim(extended, 3 - offset, 3 - offset + count, axis=0)
        keep = (lax.slice_in_dim(owners, 3 - offset, 3 - offset + count, axis=0) == current).astype(
            jnp.float32
        )
        total = total + kernel[offset] * earlier * keep[:, None, None]
    return jax.nn.silu(total)


def prepare(extended, small, kernel, rate, owners):
    mixed = short_conv(extended, owners, kernel)
    rows_here, heads, channels = mixed.shape
    width = channels // (1 + 2 * HOUSE)
    queries = unit_rows(mixed[:, :, :width])
    keys = unit_rows(
        mixed[:, :, width : width * (1 + HOUSE)].reshape(rows_here, heads, HOUSE, width)
    )
    values = mixed[:, :, width * (1 + HOUSE) :].reshape(rows_here, heads, HOUSE, width)
    logits = small.reshape(rows_here, heads, HOUSE + 1)
    betas = 2.0 * jax.nn.sigmoid(logits[:, :, :HOUSE])
    log_decay = -rate[None, :] * jax.nn.softplus(logits[:, :, HOUSE])
    return (queries, keys, values, betas, log_decay)


def solve_lower(system, right):
    return jax.scipy.linalg.solve_triangular(system, right, lower=True, unit_diagonal=True)


def compose(earlier, later):
    joined_map = jnp.einsum("...de,...ef->...df", later[0], earlier[0], precision=FULL_PRECISION)
    joined_add = (
        jnp.einsum("...de,...ef->...df", later[0], earlier[1], precision=FULL_PRECISION) + later[1]
    )
    return (joined_map, joined_add)


def group_terms(queries, keys, values, betas, log_decay, owners, owner_before):
    rows_here, heads, house, width = keys.shape
    blocks = rows_here // GROUP
    micro = GROUP * house

    def regroup(array):
        array = array.reshape((blocks, GROUP) + array.shape[1:])
        array = jnp.swapaxes(array, 1, 2)
        return array.reshape((blocks, heads, micro) + array.shape[4:])

    key_steps = regroup(keys)
    value_steps = regroup(values)
    beta_steps = regroup(betas)
    padding = jnp.zeros((rows_here, heads, house - 1), jnp.float32)
    gate_steps = regroup(jnp.concatenate([log_decay[:, :, None], padding], axis=2))
    owner_blocks = owners.reshape(blocks, GROUP)
    owner_steps = jnp.repeat(owner_blocks, house, axis=1)
    owner_prior = jnp.concatenate([jnp.reshape(owner_before, (1,)), owner_blocks[:-1, -1]])
    query_blocks = jnp.swapaxes(queries.reshape(blocks, GROUP, heads, width), 1, 2)
    cumulative = jnp.cumsum(gate_steps, axis=-1)
    order = jnp.arange(micro)
    same = owner_steps[:, :, None] == owner_steps[:, None, :]
    reach_mask = (order[None, :] <= order[:, None])[None] & same
    spread = jnp.minimum(cumulative[..., :, None] - cumulative[..., None, :], 0.0)
    decay = jnp.where(reach_mask[:, None], jnp.exp(spread), 0.0)
    inner = jnp.einsum("bhmd,bhid->bhmi", key_steps, key_steps, precision=FULL_PRECISION)
    strict = order[None, :] < order[:, None]
    lower_part = jnp.where(strict, decay * inner * beta_steps[..., :, None], 0.0)
    system = lower_part + jnp.eye(micro, dtype=jnp.float32)
    carries = (owner_steps == owner_prior[:, None]).astype(jnp.float32)
    growth = jnp.exp(cumulative) * carries[:, None, :]
    plain_value_rows = solve_lower(system, beta_steps[..., None] * value_steps)
    state_pullback = solve_lower(system, (beta_steps * growth)[..., None] * key_steps)
    scores = decay[:, :, house - 1 :: house, :] * jnp.einsum(
        "bhtd,bhid->bhti", query_blocks, key_steps, precision=FULL_PRECISION
    )
    query_state = growth[:, :, house - 1 :: house, None] * query_blocks
    carried_keys = decay[:, :, -1, :, None] * key_steps
    transfer = growth[:, :, -1, None, None] * jnp.eye(width, dtype=jnp.float32) - jnp.einsum(
        "bhmd,bhme->bhde", carried_keys, state_pullback, precision=FULL_PRECISION
    )
    offset = jnp.einsum("bhmd,bhme->bhde", carried_keys, plain_value_rows, precision=FULL_PRECISION)
    return (scores, query_state, plain_value_rows, state_pullback, transfer, offset)


def group_prefix_terms(queries, keys, values, betas, log_decay, owners, owner_before):
    scores, query_state, plain_value_rows, state_pullback, transfer, offset = group_terms(
        queries, keys, values, betas, log_decay, owners, owner_before
    )
    total_map, total_add = lax.associative_scan(compose, (transfer, offset), axis=0)
    identity = jnp.broadcast_to(jnp.eye(transfer.shape[-1], dtype=jnp.float32), transfer.shape[1:])
    before_map = jnp.concatenate([identity[None], total_map[:-1]], axis=0)
    before_add = jnp.concatenate([jnp.zeros_like(offset[:1]), total_add[:-1]], axis=0)
    return (
        scores,
        query_state,
        plain_value_rows,
        state_pullback,
        before_map,
        before_add,
        total_map[-1],
        total_add[-1],
    )


def apply_state(
    scores,
    query_state,
    plain_value_rows,
    state_pullback,
    before_map,
    before_add,
    last_map,
    last_add,
    state_in,
):
    starts = (
        jnp.einsum("bhde,hef->bhdf", before_map, state_in, precision=FULL_PRECISION) + before_add
    )
    pullback_result = plain_value_rows - jnp.einsum(
        "bhmd,bhde->bhme", state_pullback, starts, precision=FULL_PRECISION
    )
    outputs = jnp.einsum(
        "bhtd,bhde->bhte", query_state, starts, precision=FULL_PRECISION
    ) + jnp.einsum("bhti,bhie->bhte", scores, pullback_result, precision=FULL_PRECISION)
    state_out = jnp.einsum("hde,hef->hdf", last_map, state_in, precision=FULL_PRECISION) + last_add
    blocks, heads, length, width = outputs.shape
    return (jnp.swapaxes(outputs, 1, 2).reshape(blocks * length, heads, width), state_out)


def gated_output(outputs, gate_part, gain_heads):
    normed = (
        outputs
        * lax.rsqrt(jnp.mean(outputs * outputs, axis=-1, keepdims=True) + EPSILON)
        * gain_heads
    )
    return normed * jax.nn.silu(gate_part)


def head_total(values):
    return lax.psum(values, "head")


def full_rows(values):
    return lax.all_gather(values, "head", axis=1, tiled=True)


def column_sum(values):
    return lax.psum_scatter(
        values.astype(jnp.bfloat16), "head", scatter_dimension=1, tiled=True
    ).astype(jnp.float32)


def norm_back(grad_normed, values, scale, gain, model_width):
    weighted = grad_normed * gain
    inner = head_total(jnp.sum(weighted * values, axis=1))
    grad_values = (
        scale[:, None] * weighted - values * (scale * scale * scale * inner / model_width)[:, None]
    )
    grad_gain = jnp.sum(grad_normed * values * scale[:, None], axis=0)
    return (grad_values, grad_gain)


def on_device(
    inputs,
    lengths,
    norm1_gain,
    w_in,
    w_small,
    conv_weight,
    decay_rate,
    out_gain,
    w_out,
    norm2_gain,
    w_gate,
    w_up,
    w_down,
    cotangent,
):
    gathered = (
        lax.all_gather(norm1_gain, "seq", axis=0, tiled=True),
        lax.all_gather(w_in, "seq", axis=0, tiled=True),
        lax.all_gather(w_small, "seq", axis=0, tiled=True),
        lax.all_gather(conv_weight, "seq", axis=1, tiled=True),
        lax.all_gather(out_gain, "seq", axis=0, tiled=True),
        lax.all_gather(w_out, "seq", axis=1, tiled=True),
        lax.all_gather(norm2_gain, "seq", axis=0, tiled=True),
        lax.all_gather(w_gate, "seq", axis=0, tiled=True),
        lax.all_gather(w_up, "seq", axis=0, tiled=True),
        lax.all_gather(w_down, "seq", axis=1, tiled=True),
    )
    gain_one = gathered[0].astype(jnp.float32)
    proj_in = gathered[1]
    proj_small = gathered[2]
    proj_out = gathered[5]
    gain_two = gathered[6].astype(jnp.float32)
    gate_in = gathered[7]
    up_in = gathered[8]
    down_out = gathered[9]
    rows_here = inputs.shape[0]
    heads = decay_rate.shape[0]
    model_width = proj_in.shape[0]
    kernel = gathered[3].astype(jnp.float32).reshape(4, heads, -1)
    channels = kernel.shape[2]
    gain_heads = gathered[4].astype(jnp.float32).reshape(heads, -1)
    head_width = gain_heads.shape[1]
    first = lax.axis_index("seq") * rows_here
    positions = first + jnp.arange(-3, rows_here, dtype=jnp.int32)
    owners = document_of(positions, lengths)
    columns = inputs.astype(jnp.float32)
    scale_one = lax.rsqrt(head_total(jnp.sum(columns * columns, axis=1)) / model_width + EPSILON)
    rows_one = full_rows((columns * scale_one[:, None] * gain_one).astype(jnp.bfloat16))
    projected = jnp.dot(rows_one, proj_in, preferred_element_type=jnp.float32).reshape(
        rows_here, heads, -1
    )
    small = jnp.dot(rows_one, proj_small, preferred_element_type=jnp.float32)
    conv_part = projected[:, :, :channels]
    gate_part = projected[:, :, channels:]
    rim = passed_along(conv_part[-3:], "seq", 1)
    extended = jnp.concatenate([rim, conv_part], axis=0)
    mixer_inputs, prepare_back = jax.vjp(
        partial(prepare, owners=owners), extended, small, kernel, decay_rate
    )
    terms, terms_back = jax.vjp(
        partial(group_prefix_terms, owners=owners[3:], owner_before=owners[2]),
        mixer_inputs[0],
        mixer_inputs[1],
        mixer_inputs[2],
        mixer_inputs[3],
        mixer_inputs[4],
    )
    last_map = terms[6]
    last_add = terms[7]

    def relay_turn(turn, state):
        moved = jnp.einsum("hde,hef->hdf", last_map, state, precision=FULL_PRECISION) + last_add
        return passed_along(moved.astype(jnp.bfloat16), "seq", 1).astype(moved.dtype)

    state_in = lax.fori_loop(0, lax.axis_size("seq") - 1, relay_turn, jnp.zeros_like(last_add))
    mixed_state, apply_back = jax.vjp(
        apply_state,
        terms[0],
        terms[1],
        terms[2],
        terms[3],
        terms[4],
        terms[5],
        terms[6],
        terms[7],
        state_in,
    )
    gated_full, gated_gradient_rows = jax.vjp(gated_output, mixed_state[0], gate_part, gain_heads)
    gated = gated_full.reshape(rows_here, -1).astype(jnp.bfloat16)
    hidden_one = columns + column_sum(jnp.dot(gated, proj_out, preferred_element_type=jnp.float32))
    scale_two = lax.rsqrt(
        head_total(jnp.sum(hidden_one * hidden_one, axis=1)) / model_width + EPSILON
    )
    rows_two = full_rows((hidden_one * scale_two[:, None] * gain_two).astype(jnp.bfloat16))
    gate_pre = jnp.dot(rows_two, gate_in, preferred_element_type=jnp.float32)
    up_pre = jnp.dot(rows_two, up_in, preferred_element_type=jnp.float32)
    sigmoid_gate = jax.nn.sigmoid(gate_pre)
    inner = (gate_pre * sigmoid_gate * up_pre).astype(jnp.bfloat16)
    output = (
        hidden_one + column_sum(jnp.dot(inner, down_out, preferred_element_type=jnp.float32))
    ).astype(jnp.bfloat16)
    grad_top = cotangent.astype(jnp.float32)
    grad_rows_two = full_rows(cotangent)
    grad_inner = jnp.dot(grad_rows_two, down_out.T, preferred_element_type=jnp.float32)
    grad_down = jnp.dot(inner.T, grad_rows_two, preferred_element_type=jnp.float32)
    grad_gate = (
        grad_inner * up_pre * sigmoid_gate * (1.0 + gate_pre * (1.0 - sigmoid_gate))
    ).astype(jnp.bfloat16)
    grad_up = (grad_inner * gate_pre * sigmoid_gate).astype(jnp.bfloat16)
    grad_gate_in = jnp.dot(rows_two.T, grad_gate, preferred_element_type=jnp.float32)
    grad_up_in = jnp.dot(rows_two.T, grad_up, preferred_element_type=jnp.float32)
    grad_normed_two = column_sum(
        jnp.dot(grad_gate, gate_in.T, preferred_element_type=jnp.float32)
        + jnp.dot(grad_up, up_in.T, preferred_element_type=jnp.float32)
    )
    grad_hidden, grad_gain_two = norm_back(
        grad_normed_two, hidden_one, scale_two, gain_two, model_width
    )
    grad_hidden = grad_hidden + grad_top
    grad_branch = full_rows(grad_hidden.astype(jnp.bfloat16))
    grad_gated = jnp.dot(grad_branch, proj_out.T, preferred_element_type=jnp.float32)
    grad_proj_out = jnp.dot(gated.T, grad_branch, preferred_element_type=jnp.float32)
    grad_outputs, grad_gate_part, grad_gain_heads = gated_gradient_rows(
        grad_gated.reshape(rows_here, heads, head_width)
    )
    blank = jnp.zeros_like(state_in)
    residual = apply_back((grad_outputs, blank))[8]
    flipped = jnp.swapaxes(last_map, 1, 2)

    def adjoint_turn(turn, adjoint):
        moved = jnp.einsum("hde,hef->hdf", flipped, adjoint, precision=FULL_PRECISION) + residual
        return passed_along(moved.astype(jnp.bfloat16), "seq", -1).astype(moved.dtype)

    grad_state = lax.fori_loop(0, lax.axis_size("seq") - 1, adjoint_turn, blank)
    state_grads = apply_back((grad_outputs, grad_state))
    input_grads = terms_back(
        (
            state_grads[0],
            state_grads[1],
            state_grads[2],
            state_grads[3],
            state_grads[4],
            state_grads[5],
            state_grads[6],
            state_grads[7],
        )
    )
    grad_extended, grad_small, grad_kernel, grad_rate = prepare_back(input_grads)
    returned_values = passed_along(grad_extended[:3], "seq", -1)
    grad_conv = grad_extended[3:] + jnp.concatenate(
        [jnp.zeros((rows_here - 3, heads, channels), jnp.float32), returned_values], axis=0
    )
    grad_projected = (
        jnp.concatenate([grad_conv, grad_gate_part], axis=2)
        .reshape(rows_here, -1)
        .astype(jnp.bfloat16)
    )
    grad_small_low = grad_small.astype(jnp.bfloat16)
    gradient_input_projection = jnp.dot(
        rows_one.T, grad_projected, preferred_element_type=jnp.float32
    )
    grad_proj_small = jnp.dot(rows_one.T, grad_small_low, preferred_element_type=jnp.float32)
    grad_normed_one = column_sum(
        jnp.dot(grad_projected, proj_in.T, preferred_element_type=jnp.float32)
        + jnp.dot(grad_small_low, proj_small.T, preferred_element_type=jnp.float32)
    )
    grad_columns, grad_gain_one = norm_back(
        grad_normed_one, columns, scale_one, gain_one, model_width
    )
    grad_inputs = grad_columns + grad_hidden
    grad_rate_all = lax.psum(grad_rate, "seq")
    sums = (
        lax.psum_scatter(
            grad_gain_one.astype(jnp.bfloat16), "seq", scatter_dimension=0, tiled=True
        ).astype(jnp.float32),
        lax.psum_scatter(
            gradient_input_projection.astype(jnp.bfloat16), "seq", scatter_dimension=0, tiled=True
        ).astype(jnp.float32),
        lax.psum_scatter(
            grad_proj_small.astype(jnp.bfloat16), "seq", scatter_dimension=0, tiled=True
        ).astype(jnp.float32),
        lax.psum_scatter(
            grad_kernel.reshape(4, -1).astype(jnp.bfloat16), "seq", scatter_dimension=1, tiled=True
        ).astype(jnp.float32),
        lax.psum_scatter(
            grad_gain_heads.reshape(-1).astype(jnp.bfloat16), "seq", scatter_dimension=0, tiled=True
        ).astype(jnp.float32),
        lax.psum_scatter(
            grad_proj_out.astype(jnp.bfloat16), "seq", scatter_dimension=1, tiled=True
        ).astype(jnp.float32),
        lax.psum_scatter(
            grad_gain_two.astype(jnp.bfloat16), "seq", scatter_dimension=0, tiled=True
        ).astype(jnp.float32),
        lax.psum_scatter(
            grad_gate_in.astype(jnp.bfloat16), "seq", scatter_dimension=0, tiled=True
        ).astype(jnp.float32),
        lax.psum_scatter(
            grad_up_in.astype(jnp.bfloat16), "seq", scatter_dimension=0, tiled=True
        ).astype(jnp.float32),
        lax.psum_scatter(
            grad_down.astype(jnp.bfloat16), "seq", scatter_dimension=1, tiled=True
        ).astype(jnp.float32),
    )
    return (
        output,
        grad_inputs,
        sums[0],
        sums[1],
        sums[2],
        sums[3],
        grad_rate_all,
        sums[4],
        sums[5],
        sums[6],
        sums[7],
        sums[8],
        sums[9],
    )


def solution(mesh):
    return jax.shard_map(
        on_device,
        mesh=mesh,
        in_specs=(
            P("seq", "head"),
            P(),
            P(("head", "seq")),
            P("seq", "head"),
            P("seq", "head"),
            P(None, ("head", "seq")),
            P("head"),
            P(("head", "seq")),
            P("head", "seq"),
            P(("head", "seq")),
            P("seq", "head"),
            P("seq", "head"),
            P("head", "seq"),
            P("seq", "head"),
        ),
        out_specs=(
            P("seq", "head"),
            P("seq", "head"),
            P(("head", "seq")),
            P("seq", "head"),
            P("seq", "head"),
            P(None, ("head", "seq")),
            P("head"),
            P(("head", "seq")),
            P("head", "seq"),
            P(("head", "seq")),
            P("seq", "head"),
            P("seq", "head"),
            P("head", "seq"),
        ),
        check_vma=False,
    )
```

profile of v0, /device:TPU:0, one launch (start us, length us, event | category | flops | bytes accessed | tf_op | source)
XLA Modules:
  0.0 1417.0 jit_solution(10426307552155913697)
XLA Ops:
  11.8 23.6 %all-reduce.67 = (bf16[256]{0:T(256)(128)(2,1)S(1)}, bf16[256]{0:T(256)(128)(2,1)S(1)}, bf16[256]{0:T(256)(128)(2,1)}) all-reduce(bf16[256]{0:T(256)(128)(2,1)S(1)} %dynamic-update-slice, bf16[256]{0:T(256)(128)(2,1)S(1)} %dynamic-update-slice.1, bf16[256]{0:T(256)(128)(2,1)S(1)} %dynamic-update-slice.2), channel_id=1, replica_groups=mesh['seq'=8,'head'=4] {'seq'}, use_global_device_ids=true, to_apply=%add.60 | all-reduce | flops 768 | bytes 3072
  46.4 26.1 %all-gather = bf16[8,160,4]{1,2,0:T(4,128)(2,1)S(1)} all-gather(bf16[1,160,4]{1,2,0:T(4,128)(2,1)} %bitcast.466), channel_id=1, replica_groups=mesh['seq'=8,'head'=4] {'seq'}, dimensions={0}, use_global_device_ids=true | all-gather | bytes 11520 | tf_op jit(solution)/shard_map/all_gather | solution.py:214
  73.7 26.4 %all_gather.44 = bf16[1024,6]{0,1:T(8,128)(2,1)S(1)} all-gather(bf16[128,6]{0,1:T(8,128)(2,1)} %param.26), channel_id=1, replica_groups=mesh['seq'=8,'head'=4] {'seq'}, dimensions={0}, use_global_device_ids=true | all-gather | bytes 13824 | tf_op jit(solution)/shard_map/all_gather | solution.py:213
  102.7 30.6 %all_gather.48 = bf16[256,1024]{1,0:T(8,128)(2,1)} all-gather(bf16[256,128]{1,0:T(8,128)(2,1)} %param.30), channel_id=1, replica_groups=mesh['seq'=8,'head'=4] {'seq'}, dimensions={1}, use_global_device_ids=true | all-gather | bytes 589824 | tf_op jit(solution)/shard_map/all_gather | solution.py:216
  176.8 158.2 %custom-call.12 = f32[8,2,1,128,128]{3,4,2,1,0:T(8,128)S(1)} custom-call(f32[8,2,1,128,128]{4,3,2,1,0:T(8,128)} %get-tuple-element.212), custom_call_target="InvertDiagBlocksLowerTriangular" | custom-call | tf_op jit(solution)/shard_map/jvp(jit(_solve_triangular))/vmap(vmap())/triangular_solve | solution.py:60
  428.6 59.5 %while.22 = (s32[]{:T(128)}, f32[2,128,128]{2,1,0:T(8,128)S(1)}, f32[2,128,128]{2,1,0:T(8,128)S(1)}, f32[2,128,128]{2,1,0:T(8,128)S(1)}, s32[]{:T(128)}, /*index=5*/s32[]{:T(128)}) while((s32[]{:T(128)}, f32[2,128,128]{2,1,0:T(8,128)S(1)}, f32[2,128,128]{2,1,0:T(8,128)S(1)}, f32[2,128,128]{2,1,0:T(8,128)S(1)}, s32[]{:T(128)}, ...), condition=%wide.region_8.10_spmd.clone, body=%wide.region_7.9_spmd.clone.sunk | while | flops 50462720 | bytes 917623 | solution.py:269
  470.8 5.8 collective-permute-start
  479.9 5.8 collective-permute-start
  508.7 27.7 %reduce-scatter.24.cloned.1.call-done = bf16[512,256]{1,0:T(8,128)(2,1)} async-done(((bf16[512,1024]{1,0:T(8,128)(2,1)}), bf16[512,256]{1,0:T(8,128)(2,1)}) %reduce-scatter.24.cloned.1.call-update) | async-done | bytes 262160 | tf_op jit(solution)/shard_map/reduce_scatter | solution.py:179
  547.7 34.7 %all-gather.16.cloned.1.call-done = bf16[1024,704]{0,1:T(8,128)(2,1)} async-done(((bf16[128,704]{0,1:T(8,128)(2,1)}), bf16[1024,704]{0,1:T(8,128)(2,1)}) %all-gather.16.cloned.1.call-update) | async-done | bytes 1441808 | tf_op jit(solution)/shard_map/all_gather | solution.py:218
  582.3 17.3 %all-gather.14.cloned.1.call-done = bf16[512,1024]{1,0:T(8,128)(2,1)} async-done(((bf16[512,256]{1,0:T(8,128)(2,1)}), bf16[512,1024]{1,0:T(8,128)(2,1)}) %all-gather.14.cloned.1.call-update) | async-done | bytes 1048592 | tf_op jit(solution)/shard_map/all_gather | solution.py:175
  603.4 42.2 %all-gather.18.cloned.1.call-done = bf16[1024,704]{0,1:T(8,128)(2,1)} async-done(((bf16[128,704]{0,1:T(8,128)(2,1)}), bf16[1024,704]{0,1:T(8,128)(2,1)}) %all-gather.18.cloned.1.call-update) | async-done | bytes 1441808 | tf_op jit(solution)/shard_map/all_gather | solution.py:219
  649.4 13.2 all-gather.22.cloned.1.call-done
  662.5 46.1 %all-gather.20.cloned.1.call-done = bf16[704,1024]{1,0:T(8,128)(2,1)} async-done(((bf16[704,128]{1,0:T(8,128)(2,1)}), bf16[704,1024]{1,0:T(8,128)(2,1)}) %all-gather.20.cloned.1.call-update) | async-done | bytes 1441808 | tf_op jit(solution)/shard_map/all_gather | solution.py:220
  717.6 23.4 %reduce-scatter.28.cloned.1.call-done = bf16[512,256]{1,0:T(8,128)(2,1)} async-done(((bf16[512,1024]{1,0:T(8,128)(2,1)}), bf16[512,256]{1,0:T(8,128)(2,1)}) %reduce-scatter.28.cloned.1.call-update) | async-done | bytes 262160 | tf_op jit(solution)/shard_map/reduce_scatter | solution.py:179
  802.0 77.5 %while.23 = (s32[]{:T(128)}, f32[2,128,128]{2,1,0:T(8,128)}, f32[2,128,128]{2,1,0:T(8,128)}, f32[2,128,128]{2,1,0:T(8,128)}, s32[]{:T(128)}, /*index=5*/s32[]{:T(128)}) while((s32[]{:T(128)}, f32[2,128,128]{2,1,0:T(8,128)}, f32[2,128,128]{2,1,0:T(8,128)}, f32[2,128,128]{2,1,0:T(8,128)}, s32[]{:T(128)}, ...), condition=%wide.region_19.21_spmd.clone, body=%wide.region_18.20_spmd.clone.sunk | while | flops 50462720 | bytes 917623 | solution.py:328
  825.6 6.1 collective-permute-done.1
  836.4 6.4 collective-permute-done.1
  847.5 6.1 collective-permute-done.1
  858.3 8.0 collective-permute-done.1
  871.0 7.0 collective-permute-done.1
  981.9 5.9 pad.282
  1009.7 9.5 pad.292
  1085.7 6.3 pad_add_fusion
  1116.9 21.1 %psum.39 = f32[2]{0:T(128)} all-reduce(f32[2]{0:T(128)S(1)} %neg.61), channel_id=1, replica_groups=mesh['seq'=8,'head'=4] {'seq'}, use_global_device_ids=true, to_apply=%region_44.47 | all-reduce | flops 2 | bytes 16 | tf_op jit(solution)/shard_map/psum | solution.py:365
  1138.0 9.4 reduce-scatter.36.cloned.1.call-done
  1148.9 62.3 %reduce-scatter.34.cloned.1.call-done = bf16[128,6]{1,0:T(8,128)(2,1)} async-done(((bf16[1024,6]{1,0:T(8,128)(2,1)}), bf16[128,6]{1,0:T(8,128)(2,1)}) %reduce-scatter.34.cloned.1.call-update) | async-done | bytes 1552
  1212.6 63.7 %reduce-scatter.38.cloned.1.call-done = bf16[128,256]{1,0:T(8,128)(2,1)} async-done(((bf16[1024,256]{1,0:T(8,128)(2,1)}), bf16[128,256]{1,0:T(8,128)(2,1)}) %reduce-scatter.38.cloned.1.call-update) | async-done | bytes 65552
  1277.9 24.7 %reduce-scatter.30.cloned.1.call-done = bf16[512,256]{1,0:T(8,128)(2,1)} async-done(((bf16[512,1024]{1,0:T(8,128)(2,1)}), bf16[512,256]{1,0:T(8,128)(2,1)}) %reduce-scatter.30.cloned.1.call-update) | async-done | bytes 262160 | tf_op jit(solution)/shard_map/reduce_scatter | solution.py:179
  1303.9 21.4 %all-reduce.66 = (bf16[256]{0:T(256)(128)(2,1)S(1)}, bf16[256]{0:T(256)(128)(2,1)S(1)}, bf16[256]{0:T(256)(128)(2,1)S(1)}) all-reduce(bf16[256]{0:T(256)(128)(2,1)S(1)} %get-tuple-element.142, bf16[256]{0:T(256)(128)(2,1)S(1)} %bitcast.467, bf16[256]{0:T(256)(128)(2,1)S(1)} %copy-done.192), channel_id=6, replica_groups=mesh['seq'=8,'head'=4] {'seq'}, use_global_device_ids=true, to_apply=%region_35.38.clone | all-reduce | flops 768 | bytes 3072
  1325.3 5.9 psum.38
  1335.3 73.0 %reduce-scatter.32.cloned.1.call-done = bf16[128,1536]{1,0:T(8,128)(2,1)} async-done(((bf16[1024,1536]{1,0:T(8,128)(2,1)}), bf16[128,1536]{1,0:T(8,128)(2,1)}) %reduce-scatter.32.cloned.1.call-update) | async-done | bytes 393232 | tf_op jit(solution)/shard_map/reduce_scatter | solution.py:370
  (824 shorter events, 580.5 us)
Async XLA Ops:
  7.2 126.1 %all-gather.10.cloned.1.call-start = ((), (), s32[]{:S(2)}) async-start(), calls=%async_computation.11 | async-start | bytes 1310720 | tf_op jit(solution)/shard_map/all_gather | solution.py:175
  44.0 92.8 %all-gather.12.cloned.1.call-start = ((), (), s32[]{:S(2)}) async-start(), calls=%async_computation.12 | async-start | bytes 3538944 | tf_op jit(solution)/shard_map/all_gather | solution.py:212
  44.7 491.7 %reduce-scatter.24.cloned.1.call-start = ((), (), s32[]{:S(2)}) async-start(), calls=%async_computation.13 | async-start | bytes 1310720 | tf_op jit(solution)/shard_map/reduce_scatter | solution.py:179
  148.5 10.0 collective-permute-start.2
  437.5 6.5 collective-permute-start
  445.7 6.5 collective-permute-start
  462.2 6.8 collective-permute-start
  470.8 7.4 collective-permute-start
  479.9 7.4 collective-permute-start
  508.1 74.3 %all-gather.16.cloned.1.call-start = ((), (), s32[]{:S(2)}) async-start(), calls=%async_computation.15 | async-start | bytes 1622016 | tf_op jit(solution)/shard_map/all_gather | solution.py:218
  508.7 91.0 %all-gather.14.cloned.1.call-start = ((), (), s32[]{:S(2)}) async-start(), calls=%async_computation.14 | async-start | bytes 1310720 | tf_op jit(solution)/shard_map/all_gather | solution.py:175
  545.1 100.5 %all-gather.18.cloned.1.call-start = ((), (), s32[]{:S(2)}) async-start(), calls=%async_computation.16 | async-start | bytes 1622016 | tf_op jit(solution)/shard_map/all_gather | solution.py:219
  545.7 116.8 %all-gather.22.cloned.1.call-start = ((), (), s32[]{:S(2)}) async-start(), calls=%async_computation.19 | async-start | bytes 1310720 | tf_op jit(solution)/shard_map/all_gather | solution.py:175
  546.5 162.2 %all-gather.20.cloned.1.call-start = ((), (), s32[]{:S(2)}) async-start(), calls=%async_computation.17 | async-start | bytes 1622016 | tf_op jit(solution)/shard_map/all_gather | solution.py:220
  547.2 193.8 %reduce-scatter.28.cloned.1.call-start = ((), (), s32[]{:S(2)}) async-start(), calls=%async_computation.20 | async-start | bytes 1310720 | tf_op jit(solution)/shard_map/reduce_scatter | solution.py:179
  717.6 63.1 %all-gather.24.cloned.1.call-start = ((), (), s32[]{:S(2)}) async-start(), calls=%async_computation.21 | async-start | bytes 1310720 | tf_op jit(solution)/shard_map/all_gather | solution.py:175
  750.7 360.5 %reduce-scatter.40.cloned.1.call-start = ((), (), s32[]{:S(2)}) async-start(), calls=%async_computation.27 | async-start | bytes 1769472
  756.8 356.2 %reduce-scatter.42.cloned.1.call-start = ((), (), s32[]{:S(2)}) async-start(), calls=%async_computation.28 | async-start | bytes 1769472
  763.1 351.8 %reduce-scatter.44.cloned.1.call-start = ((), (), s32[]{:S(2)}) async-start(), calls=%async_computation.29 | async-start | bytes 1769472
  780.4 367.0 %reduce-scatter.36.cloned.1.call-start = ((), (), s32[]{:S(2)}) async-start(), calls=%async_computation.25 | async-start | bytes 368640
  813.9 7.0 collective-permute-start.1
  824.3 7.4 collective-permute-start.1
  835.1 7.7 collective-permute-start.1
  846.2 7.4 collective-permute-start.1
  857.0 9.3 collective-permute-start.1
  869.7 8.3 collective-permute-start.1
  1082.7 10.4 collective-permute-start.3
  1084.0 127.2 %reduce-scatter.34.cloned.1.call-start = ((), (), s32[]{:S(2)}) async-start(), calls=%async_computation.24 | async-start | bytes 294912
  1085.2 191.1 %reduce-scatter.38.cloned.1.call-start = ((), (), s32[]{:S(2)}) async-start(), calls=%async_computation.26 | async-start | bytes 589824
  1093.1 209.5 %reduce-scatter.30.cloned.1.call-start = ((), (), s32[]{:S(2)}) async-start(), calls=%async_computation.22 | async-start | bytes 1310720 | tf_op jit(solution)/shard_map/reduce_scatter | solution.py:179
  1102.9 230.1 %reduce-scatter.26.cloned.1.call-start = ((), (), s32[]{:S(2)}) async-start(), calls=%async_computation.18 | async-start | bytes 1310720 | tf_op jit(solution)/shard_map/reduce_scatter | solution.py:179
  1106.7 301.6 %reduce-scatter.32.cloned.1.call-start = ((), (), s32[]{:S(2)}) async-start(), calls=%async_computation.23 | async-start | bytes 3538944 | tf_op jit(solution)/shard_map/reduce_scatter | solution.py:370
  (207 other events, 5276.1 us)
Sparse Core Ops, SparseCore 0:
  44.1 14.3 all-gather.9
  60.7 65.5 all-gather.11
  508.2 28.1 reduce-scatter.23
  538.5 43.8 all-gather.15
  584.4 15.2 all-gather.13
  601.8 43.8 all-gather.17
  647.2 15.2 all-gather.21
  664.7 43.8 all-gather.19
  717.7 23.2 reduce-scatter.27
  750.8 17.9 all-gather.23
  772.2 65.3 reduce-scatter.39
  841.3 63.1 reduce-scatter.41
  907.9 63.6 reduce-scatter.43
  1084.1 63.2 reduce-scatter.35
  1150.9 60.1 reduce-scatter.33
  1215.3 60.9 reduce-scatter.37
  1278.7 23.9 reduce-scatter.29
  1305.2 24.9 reduce-scatter.25
  1333.7 74.5 reduce-scatter.31
where the time goes:
time: 1430 us; the launch traced here: 1420 us
  waiting for transfers between devices  497 us (35%)
  other arithmetic  272 us (19%)
  local copies, waits for them, and re-layouts  209 us (15%)
  matrix products  198 us (14%)
  blocking collectives  172 us (12%)
  starting transfers between devices  50.2 us (4%)
  between operations  18.3 us (1%)
    another operation x3, other arithmetic, solve_lower(): jax.scipy.linalg.solve_triangular(system, right, lower=True, unit_diagona...  158 us
    unnamed x25, waiting for transfers between devices  139 us
    reduce_scatter x4, waiting for transfers between devices, column_sum(): lax.psum_scatter(values.astype(jnp.bfloat16), 'head', scatter_dimension=1...  75.8 us
    pad x19, local copies, waits for them, and re-layouts, group_prefix_terms(): lax.associative_scan(compose, (transfer, offset), axis=0)  75.5 us
    reduce_scatter x1, waiting for transfers between devices, on_device(): lax.psum_scatter(gradient_input_projection.astype(jnp.bfloat16), 'seq', s...  73 us
    ppermute x16, waiting for transfers between devices, passed_along(): lax.ppermute(value, axis, [(source, source + steps) for source in range(i...  55.5 us
    ppermute x16, starting transfers between devices, passed_along(): lax.ppermute(value, axis, [(source, source + steps) for source in range(i...  48.8 us
    all_gather x1, waiting for transfers between devices, on_device(): lax.all_gather(w_down, 'seq', axis=1, tiled=True)  46.1 us
  transfers between devices with their start and end apart: 35, of which 26 were waited for; matrix products, arithmetic and copies ran while one was open for 24% of the time, Pallas kernels for 0%

commit v1 on v0

v1 whole, which is shorter than its diff:
```python
from functools import partial

import jax
import jax.numpy as jnp
from jax import lax
from jax.experimental import pallas as pl
from jax.experimental.pallas import tpu as pltpu
from jax.sharding import PartitionSpec as P

HOUSE = 2
GROUP = 64
MICRO = GROUP * HOUSE
WIDTH = 128
RIM = 16
EPSILON = 1e-06
MESH = pl.DeviceIdType.MESH
VMEM_BYTES = 56 * 2**20
F32 = jnp.float32
BF16 = jnp.bfloat16

VMEM = pl.BlockSpec(memory_space=pltpu.VMEM)
SMEM = pl.BlockSpec(memory_space=pltpu.SMEM)
ANY = pl.BlockSpec(memory_space=pl.ANY)
DMA = pltpu.SemaphoreType.DMA


def shape(dims, kind):
    return jax.ShapeDtypeStruct(tuple(dims), kind)


def dot(left, right, over=(1, 0)):
    return lax.dot_general(
        left, right, (((over[0],), (over[1],)), ((), ())), preferred_element_type=F32
    )


def dot_low(left, right, over=(1, 0)):
    return dot(left.astype(BF16), right.astype(BF16), over)


def halves(values):
    high = values.astype(BF16)
    return high, (values - high.astype(F32)).astype(BF16)


def dot_mid(left, right, over=(1, 0)):
    left_high, left_low = halves(left)
    right_high, right_low = halves(right)
    return (
        dot(left_high, right_low, over)
        + dot(left_low, right_high, over)
        + dot(left_high, right_high, over)
    )


def rows_of(count):
    return lax.broadcasted_iota(jnp.int32, (count, 1), 0)


def lanes_of(count):
    return lax.broadcasted_iota(jnp.int32, (1, count), 1)


def to_lane(column):
    count = column.shape[0]
    return jnp.sum(jnp.where(rows_of(count) == lanes_of(count), column, 0.0), axis=0, keepdims=True)


def to_column(lane):
    count = lane.shape[1]
    return jnp.sum(jnp.where(rows_of(count) == lanes_of(count), lane, 0.0), axis=1, keepdims=True)


def row_sum(values):
    return jnp.sum(values, axis=1, keepdims=True)


def bounds_of(lengths_ref):
    bounds = []
    total = 0
    for at in range(lengths_ref.shape[0]):
        total = total + lengths_ref[at]
        bounds.append(total)
    return bounds


def owner_of(positions, bounds):
    total = jnp.zeros_like(positions)
    for bound in bounds:
        total = total + (bound <= positions).astype(jnp.int32)
    return total


def micro_order(index):
    return 2 * (index & (GROUP - 1)) + lax.shift_right_logical(index, 6)


def unit_inverse(lowers):
    above, left = micro_order(rows_of(MICRO)), micro_order(lanes_of(MICRO))
    eye = (rows_of(MICRO) == lanes_of(MICRO)).astype(F32)

    def level_mask(level):
        step = 1 << level
        return (
            (lax.shift_right_logical(above, level + 1) == lax.shift_right_logical(left, level + 1))
            & ((above & step) != 0)
            & ((left & step) == 0)
        )

    first = level_mask(0)
    found = [eye - jnp.where(first, lower, 0.0) for lower in lowers]
    for level in range(1, 7):
        mask = level_mask(level)
        inner = [dot_mid(jnp.where(mask, a, 0.0), b) for a, b in zip(lowers, found)]
        found = [b - dot_mid(b, a) for a, b in zip(inner, found)]
    return found


def conv_window(proj_ref, group, column):
    start = pl.multiple_of(group * GROUP + RIM - 8, 8)
    window = proj_ref[pl.ds(start, GROUP + 8), column : column + WIDTH]
    return [window[8 - step : GROUP + 8 - step] for step in range(4)]


def conv_keeps(group, first, bounds):
    positions = first + group * GROUP + rows_of(GROUP)
    current = owner_of(positions, bounds)
    return [None] + [
        (owner_of(positions - step, bounds) == current).astype(F32) for step in range(1, 4)
    ]


def conv_total(parts, keeps, taps_ref, column):
    total = parts[0] * taps_ref[0:1, column : column + WIDTH]
    for step in range(1, 4):
        total = total + parts[step] * keeps[step] * taps_ref[step : step + 1, column : column + WIDTH]
    return total


def gate_terms(small_ref, rate, group, head):
    logits = small_ref[pl.ds(pl.multiple_of(group * GROUP, GROUP), GROUP), :]
    at = head * (HOUSE + 1)
    betas = 2.0 * jax.nn.sigmoid(logits[:, at : at + HOUSE])
    decay_logit = logits[:, at + HOUSE : at + HOUSE + 1]
    soft = jnp.maximum(decay_logit, 0.0) + jnp.log(1.0 + jnp.exp(-jnp.abs(decay_logit)))
    log_decay = -rate * soft
    upto = lanes_of(GROUP) <= rows_of(GROUP)
    cumulative = row_sum(jnp.where(upto, to_lane(log_decay), 0.0))
    return betas, decay_logit, soft, cumulative


def group_masks(group, first, bounds):
    order, order_lane = micro_order(rows_of(MICRO)), micro_order(lanes_of(MICRO))
    start = first + group * GROUP
    owners = owner_of(start + (rows_of(MICRO) & (GROUP - 1)), bounds)
    owners_lane = owner_of(start + (lanes_of(MICRO) & (GROUP - 1)), bounds)
    prior = owner_of(jnp.full((1, 1), start - 1, jnp.int32), bounds)
    last = owner_of(jnp.full((1, 1), start + GROUP - 1, jnp.int32), bounds)
    same = owners == owners_lane
    reach = same & (order_lane <= order)
    strict = order_lane < order
    carries = (owners == prior).astype(F32)
    ends = owners == last
    return reach, strict, carries, ends


def decay_terms(cumulative, masks):
    reach, strict, carries, ends = masks
    column = jnp.concatenate([cumulative, cumulative], axis=0)
    lane = to_lane(column)
    decay = jnp.where(reach, jnp.exp(jnp.minimum(column - lane, 0.0)), 0.0)
    growth = jnp.exp(column) * carries
    final = column[MICRO - 1 : MICRO]
    to_end = jnp.where(ends, jnp.exp(jnp.minimum(final - column, 0.0)), 0.0)
    return decay, growth, to_end


def seq_links():
    me_seq, me_head = lax.axis_index("seq"), lax.axis_index("head")
    outer = lax.axis_size("seq") // 2
    place, inner = me_seq // 2, lax.rem(me_seq, 2)
    return me_seq, me_head, outer, place, inner


def other_of(index):
    return index + 1 - 2 * lax.rem(index, 2)


def greet(devices):
    barrier = pltpu.get_barrier_semaphore()
    count = 0
    for condition, device in devices:
        if condition is None:
            pl.semaphore_signal(barrier, inc=1, device_id=device, device_id_type=MESH)
            count = count + 1
        else:

            @pl.when(condition)
            def _():
                pl.semaphore_signal(barrier, inc=1, device_id=device, device_id_type=MESH)

            count = count + jnp.where(condition, 1, 0)
    pl.semaphore_wait(barrier, count)


def seq_neighbours():
    me_seq, me_head, outer, place, inner = seq_links()
    return [
        (None, (other_of(me_seq), me_head)),
        (place < outer - 1, (me_seq + 2, me_head)),
        (place > 0, (me_seq - 2, me_head)),
    ]


def head_neighbours():
    me_seq, me_head = lax.axis_index("seq"), lax.axis_index("head")
    outer = lax.axis_size("head") // 2
    found = [(None, (me_seq, other_of(me_head)))]
    for step in range(1, outer):
        found.append((None, (me_seq, lax.rem(me_head + 2 * step, 2 * outer))))
    return found


def remote(source, target, send, receive, device):
    return pltpu.make_async_remote_copy(
        src_ref=source,
        dst_ref=target,
        send_sem=send,
        recv_sem=receive,
        device_id=device,
        device_id_type=MESH,
    )


class SeqGather:
    def __init__(self, source, target, sends, receives):
        self.source, self.target = source, target
        self.sends, self.receives = sends, receives

    def block(self, origin):
        return self.target.at[origin]

    def send(self, origin, way, device, source=None):
        source = self.block(origin) if source is None else source
        remote(
            source, self.block(origin), self.sends.at[origin, way], self.receives.at[origin], device
        ).start()

    def wait_send(self, origin, way):
        me_seq, me_head, outer, place, inner = seq_links()
        remote(
            self.block(origin),
            self.block(origin),
            self.sends.at[origin, way],
            self.receives.at[origin],
            (me_seq, me_head),
        ).wait_send()

    def wait_arrival(self, origin):
        me_seq, me_head, outer, place, inner = seq_links()
        remote(
            self.block(origin),
            self.block(origin),
            self.sends.at[origin, 0],
            self.receives.at[origin],
            (me_seq, me_head),
        ).wait_recv()

    def start(self, local):
        me_seq, me_head, outer, place, inner = seq_links()
        self.local = pltpu.make_async_copy(self.source, self.block(me_seq), local)
        self.local.start()

        @pl.when(place < outer - 1)
        def _():
            self.send(me_seq, 0, (me_seq + 2, me_head), self.source)

        @pl.when(place > 0)
        def _():
            self.send(me_seq, 1, (me_seq - 2, me_head), self.source)

        self.send(me_seq, 2, (other_of(me_seq), me_head), self.source)

    def relay(self, step):
        me_seq, me_head, outer, place, inner = seq_links()
        below, above = me_seq - 2 * step, me_seq + 2 * step
        aside = (other_of(me_seq), me_head)

        @pl.when(place >= step)
        def _():
            self.wait_arrival(below)

            @pl.when(place < outer - 1)
            def _():
                self.send(below, 0, (me_seq + 2, me_head))

            self.send(below, 2, aside)

        @pl.when(place < outer - step)
        def _():
            self.wait_arrival(above)

            @pl.when(place > 0)
            def _():
                self.send(above, 1, (me_seq - 2, me_head))

            self.send(above, 2, aside)

    def finish(self):
        me_seq, me_head, outer, place, inner = seq_links()
        self.local.wait()
        for at in range(outer):
            self.wait_arrival(2 * at + 1 - inner)
        for at in range(outer):
            origin = 2 * at + inner
            self.wait_send(origin, 2)

            @pl.when((at <= place) & (place < outer - 1))
            def _():
                self.wait_send(origin, 0)

            @pl.when((at >= place) & (place > 0))
            def _():
                self.wait_send(origin, 1)


class HeadGather:
    def __init__(self, source, place_of, sends, receives):
        self.source, self.place_of = source, place_of
        self.sends, self.receives = sends, receives

    def links(self):
        me_seq, me_head = lax.axis_index("seq"), lax.axis_index("head")
        return me_seq, me_head, lax.axis_size("head") // 2

    def copy(self, origin, way, device, source=None):
        target = self.place_of(origin)
        return remote(
            target if source is None else source,
            target,
            self.sends.at[origin, way],
            self.receives.at[origin],
            device,
        )

    def start(self, local=None):
        me_seq, me_head, outer = self.links()
        self.local = None
        if local is not None:
            self.local = pltpu.make_async_copy(self.source, self.place_of(me_head), local)
            self.local.start()
        for step in range(1, outer):
            device = (me_seq, lax.rem(me_head + 2 * step, 2 * outer))
            self.copy(me_head, step, device, self.source).start()
        self.copy(me_head, 0, (me_seq, other_of(me_head)), self.source).start()

    def hand_on(self):
        me_seq, me_head, outer = self.links()
        for step in range(1, outer):
            origin = lax.rem(me_head + 2 * (outer - step), 2 * outer)
            self.copy(origin, 0, (me_seq, me_head)).wait_recv()
            self.copy(origin, 0, (me_seq, other_of(me_head))).start()

    def finish(self):
        me_seq, me_head, outer = self.links()
        if self.local is not None:
            self.local.wait()
        for step in range(outer):
            origin = lax.rem(other_of(me_head) + 2 * step, 2 * outer)
            self.copy(origin, 0, (me_seq, me_head)).wait_recv()
        for step in range(outer):
            origin = lax.rem(me_head + 2 * step, 2 * outer)
            self.copy(origin, 0, (me_seq, me_head)).wait_send()
        for step in range(1, outer):
            self.copy(me_head, step, (me_seq, me_head)).wait_send()


def entry_kernel(seq_count, wide_count, *refs):
    refs = list(refs)
    take = lambda count: [refs.pop(0) for _ in range(count)]
    columns, cotangent = take(2)
    shards = take(seq_count)
    rows, grad_rows, rim = take(3)
    gathered = take(seq_count)
    wide = take(wide_count)
    head_sends, head_receives, local, rim_send, rim_receive = take(5)
    seq_sends, seq_receives = take(2)
    wide_sends, wide_receives = take(2)
    me_seq, me_head, outer, place, inner = seq_links()
    count = lax.axis_size("seq")
    after = (lax.rem(me_seq + 1, count), me_head)
    before = (lax.rem(me_seq + count - 1, count), me_head)
    greet(seq_neighbours() + head_neighbours() + [(None, after), (None, before)])
    span = columns.shape[1]

    def part_of(target):
        return lambda origin: target.at[:, pl.ds(pl.multiple_of(origin * span, span), span)]

    heads = [
        HeadGather(columns, part_of(rows), head_sends.at[0], head_receives.at[0]),
        HeadGather(cotangent, part_of(grad_rows), head_sends.at[1], head_receives.at[1]),
    ]
    gathers = [
        SeqGather(shard, target, seq_sends.at[at], seq_receives.at[at])
        for at, (shard, target) in enumerate(zip(shards, gathered))
    ]
    heads[0].start(local.at[0])
    for at, gather in enumerate(gathers):
        gather.start(local.at[2 + at])
    heads[1].start(local.at[1])
    heads[0].hand_on()
    heads[0].finish()
    tail = rows.at[pl.ds(rows.shape[0] - RIM, RIM), :]
    rim_copy = remote(tail, rim, rim_send, rim_receive, after)
    rim_copy.start()
    heads[1].hand_on()
    for step in range(1, outer):
        for gather in gathers:
            gather.relay(step)
    for gather in gathers:
        gather.finish()
    heads[1].finish()
    rim_copy.wait()
    spread = [
        HeadGather(
            gathered[at],
            (lambda origin, target=target: target.at[origin]),
            wide_sends.at[at],
            wide_receives.at[at],
        )
        for at, target in enumerate(wide)
    ]
    for at, gather in enumerate(spread):
        gather.start(local.at[2 + at])
    for gather in spread:
        gather.hand_on()
    for gather in spread:
        gather.finish()


def entry(columns, cotangent, shards, wide_count, n_seq, n_head):
    rows_here, span = columns.shape
    full = (rows_here, span * n_head)
    gathered = [shape((n_seq,) + a.shape, a.dtype) for a in shards]
    wide = [shape((n_head, n_seq) + a.shape, a.dtype) for a in shards[:wide_count]]
    count = len(shards)
    outs = pl.pallas_call(
        partial(entry_kernel, count, wide_count),
        out_shape=[shape(full, BF16), shape(full, BF16), shape((RIM, full[1]), BF16)]
        + gathered
        + wide,
        in_specs=[ANY] * (2 + count),
        out_specs=[ANY] * (3 + count + wide_count),
        scratch_shapes=[
            DMA((2, n_head, n_head // 2)),
            DMA((2, n_head)),
            DMA((2 + count,)),
            DMA,
            DMA,
            DMA((count, n_seq, 3)),
            DMA((count, n_seq)),
            DMA((wide_count, n_head, n_head // 2)),
            DMA((wide_count, n_head)),
        ],
        compiler_params=pltpu.CompilerParams(
            collective_id=0, has_side_effects=True, vmem_limit_bytes=VMEM_BYTES
        ),
        name="entry_gathers",
    )(columns, cotangent, *shards)
    return outs[0], outs[1], outs[2], outs[3 : 3 + count], outs[3 + count :]


def mixer_kernel(
    lengths_ref,
    rate_ref,
    rows_ref,
    rim_ref,
    gain_ref,
    w_in_ref,
    w_small_ref,
    taps_ref,
    normed_ref,
    proj_ref,
    small_ref,
    query_ref,
    key_ref,
    value_ref,
    inverse_ref,
    solved_ref,
    lower_ref,
    scores_ref,
    reach_ref,
    local_ref,
    map_ref,
    add_ref,
    before_ref,
    total_ref,
):
    rows_here, model = rows_ref.shape
    heads, groups = key_ref.shape[:2]
    block = proj_ref.shape[1] // heads
    me_seq = lax.axis_index("seq")
    first = me_seq * rows_here
    bounds = bounds_of(lengths_ref)

    def normed_of(values):
        values = values.astype(F32)
        scale = lax.rsqrt(row_sum(values * values) / model + EPSILON)
        return (values * scale * gain_ref[...]).astype(BF16)

    rim = jnp.where(me_seq > 0, rim_ref[...].astype(F32), 0.0)
    normed_ref[0:RIM, :] = normed_of(rim)
    proj_ref[0:RIM, :] = dot(normed_ref[0:RIM, :], w_in_ref[...])
    tile = min(128, rows_here)

    @pl.loop(0, rows_here // tile)
    def _(at):
        start = pl.multiple_of(at * tile, tile)
        normed = normed_of(rows_ref[pl.ds(start, tile), :])
        shifted = pl.multiple_of(start + RIM, RIM)
        normed_ref[pl.ds(shifted, tile), :] = normed
        proj_ref[pl.ds(shifted, tile), :] = dot(normed, w_in_ref[...])
        small_ref[pl.ds(start, tile), :] = dot(normed, w_small_ref[...])

    eye = (rows_of(MICRO) == lanes_of(MICRO)).astype(F32)
    together = 2

    @pl.loop(0, groups // together)
    def _(pair):
        units = []
        for extra in range(together):
            group = pair * together + extra
            keeps = conv_keeps(group, first, bounds)
            masks = group_masks(group, first, bounds)
            for head in range(heads):
                blocks = []
                for part in range(1 + 2 * HOUSE):
                    parts = conv_window(proj_ref, group, head * block + part * WIDTH)
                    taps = head * (1 + 2 * HOUSE) * WIDTH + part * WIDTH
                    total = conv_total(parts, keeps, taps_ref, taps)
                    mixed = total * jax.nn.sigmoid(total)
                    if part < 1 + HOUSE:
                        mixed = mixed * lax.rsqrt(row_sum(mixed * mixed) + EPSILON)
                    blocks.append(mixed)
                query = blocks[0]
                keys = jnp.concatenate(blocks[1 : 1 + HOUSE], axis=0)
                values = jnp.concatenate(blocks[1 + HOUSE :], axis=0)
                betas, _, _, cumulative = gate_terms(small_ref, rate_ref[head], group, head)
                beta = jnp.concatenate([betas[:, 0:1], betas[:, 1:2]], axis=0)
                decay, growth, to_end = decay_terms(cumulative, masks)
                inner = dot_mid(keys, keys, (1, 1))
                lower = jnp.where(masks[1], decay * inner * beta, 0.0)
                query_ref[head, group] = query
                key_ref[head, group] = keys
                value_ref[head, group] = values
                lower_ref[head, group] = lower
                units.append((head, group, query, keys, values, beta, decay, growth, to_end, lower))
        inverses = unit_inverse([unit[-1] for unit in units])
        for unit, inverse in zip(units, inverses):
            head, group, query, keys, values, beta, decay, growth, to_end, lower = unit
            right = jnp.concatenate([beta * values, (beta * growth) * keys], axis=1)
            solved = dot_mid(inverse, right)
            scores = decay[GROUP:] * dot_mid(query, keys, (1, 1))
            seen = dot_mid(scores, solved)
            carried = dot_mid(to_end * keys, solved, (0, 0))
            inverse_ref[head, group] = inverse
            solved_ref[head, group] = solved
            scores_ref[head, group] = scores
            local_ref[head, group] = seen[:, :WIDTH]
            reach_ref[head, group] = growth[GROUP:] * query - seen[:, WIDTH:]
            map_ref[head, group] = growth[MICRO - 1 : MICRO] * eye - carried[:, WIDTH:]
            add_ref[head, group] = carried[:, :WIDTH]

    for head in range(heads):
        total_ref[head] = jnp.concatenate([eye, jnp.zeros((WIDTH, WIDTH), F32)], axis=1)

    @pl.loop(0, groups)
    def _(group):
        for head in range(heads):
            so_far = total_ref[head]
            before_ref[head, group] = so_far
            joined = dot_mid(map_ref[head, group], so_far)
            added = jnp.concatenate([jnp.zeros((WIDTH, WIDTH), F32), add_ref[head, group]], axis=1)
            total_ref[head] = joined + added


def mixer(lengths, rate, rows, rim, gain, w_in, w_small, taps):
    rows_here, model = rows.shape
    heads = rate.shape[0]
    groups = rows_here // GROUP
    unit = (heads, groups)
    return pl.pallas_call(
        mixer_kernel,
        out_shape=[
            shape((rows_here + RIM, model), BF16),
            shape((rows_here + RIM, w_in.shape[1]), F32),
            shape((rows_here, WIDTH), F32),
            shape(unit + (GROUP, WIDTH), F32),
            shape(unit + (MICRO, WIDTH), F32),
            shape(unit + (MICRO, WIDTH), F32),
            shape(unit + (MICRO, MICRO), F32),
            shape(unit + (MICRO, 2 * WIDTH), F32),
            shape(unit + (MICRO, MICRO), F32),
            shape(unit + (GROUP, MICRO), F32),
            shape(unit + (GROUP, WIDTH), F32),
            shape(unit + (GROUP, WIDTH), F32),
            shape(unit + (WIDTH, WIDTH), F32),
            shape(unit + (WIDTH, WIDTH), F32),
            shape(unit + (WIDTH, 2 * WIDTH), F32),
            shape((heads, WIDTH, 2 * WIDTH), F32),
        ],
        in_specs=[SMEM, SMEM] + [VMEM] * 6,
        out_specs=[VMEM] * 16,
        compiler_params=pltpu.CompilerParams(vmem_limit_bytes=VMEM_BYTES),
        name="mixer_terms",
    )(lengths, rate, rows, rim, gain, w_in, w_small, taps)


def state_kernel(total_ref, state_ref, pair_ref, aside_ref, own, theirs, moving, arriving, sems):
    me_seq, me_head, outer, place, inner = seq_links()
    heads = total_ref.shape[0]
    greet(seq_neighbours())
    own[...] = total_ref[...].astype(BF16)
    swap = remote(own, theirs, sems.at[0], sems.at[1], (other_of(me_seq), me_head))
    swap.start()
    swap.wait()
    for head in range(heads):
        mine, other = own[head].astype(F32), theirs[head].astype(F32)
        aside_ref[head] = other
        early = jnp.where(inner == 0, mine, other)
        late = jnp.where(inner == 0, other, mine)
        joined = dot_mid(late[:, :WIDTH], early)
        zero = jnp.zeros((WIDTH, WIDTH), F32)
        pair_ref[head] = joined + jnp.concatenate([zero, late[:, WIDTH:]], axis=1)

    step_up = remote(moving, arriving, sems.at[2], sems.at[3], (me_seq + 2, me_head))

    @pl.when(place > 0)
    def _():
        step_up.wait_recv()

    for head in range(heads):
        state = jnp.where(place > 0, arriving[head].astype(F32), 0.0)
        moved = dot_mid(pair_ref[head, :, :WIDTH], state) + pair_ref[head, :, WIDTH:]
        moving[head] = moved.astype(BF16)

    @pl.when(place < outer - 1)
    def _():
        step_up.start()

    for head in range(heads):
        state = jnp.where(place > 0, arriving[head].astype(F32), 0.0)
        stepped = dot_mid(aside_ref[head, :, :WIDTH], state) + aside_ref[head, :, WIDTH:]
        state_ref[head] = jnp.where(inner == 0, state, stepped)

    @pl.when(place < outer - 1)
    def _():
        step_up.wait_send()


def carry_state(total):
    heads = total.shape[0]
    square = (heads, WIDTH, WIDTH)
    both = (heads, WIDTH, 2 * WIDTH)
    return pl.pallas_call(
        state_kernel,
        out_shape=[shape(square, F32), shape(both, F32), shape(both, F32)],
        in_specs=[VMEM],
        out_specs=[VMEM] * 3,
        scratch_shapes=[
            pltpu.VMEM(both, BF16),
            pltpu.VMEM(both, BF16),
            pltpu.VMEM(square, BF16),
            pltpu.VMEM(square, BF16),
            DMA((4,)),
        ],
        compiler_params=pltpu.CompilerParams(
            collective_id=1, has_side_effects=True, vmem_limit_bytes=VMEM_BYTES
        ),
        name="state_relay",
    )(total)


def adjoint_kernel(
    residual_ref, pair_ref, aside_ref, adjoint_ref, own, theirs, moving, arriving, sems
):
    me_seq, me_head, outer, place, inner = seq_links()
    heads = residual_ref.shape[0]
    greet(seq_neighbours())
    own[...] = residual_ref[...].astype(BF16)
    swap = remote(own, theirs, sems.at[0], sems.at[1], (other_of(me_seq), me_head))
    swap.start()
    swap.wait()
    step_down = remote(moving, arriving, sems.at[2], sems.at[3], (me_seq - 2, me_head))

    @pl.when(place < outer - 1)
    def _():
        step_down.wait_recv()

    for head in range(heads):
        mine, other = own[head].astype(F32), theirs[head].astype(F32)
        adjoint = jnp.where(place < outer - 1, arriving[head].astype(F32), 0.0)
        late_after = jnp.where(inner == 0, other, mine)
        early_after = jnp.where(inner == 0, mine, other)
        map_other = aside_ref[head, :, :WIDTH]
        stepped = late_after + dot_mid(map_other, adjoint, (0, 0))
        adjoint_ref[head] = jnp.where(inner == 0, stepped, adjoint)
        pair_map = pair_ref[head, :, :WIDTH]
        early_map = jnp.where(inner == 0, pair_ref[head, :, WIDTH:], map_other)
        joined = early_after + dot_mid(early_map, late_after, (0, 0))
        moving[head] = (joined + dot_mid(pair_map, adjoint, (0, 0))).astype(BF16)

    @pl.when(place > 0)
    def _():
        step_down.start()
        step_down.wait_send()


def carry_adjoint(residual, pair, aside):
    heads = residual.shape[0]
    square = (heads, WIDTH, WIDTH)
    return pl.pallas_call(
        adjoint_kernel,
        out_shape=shape(square, F32),
        in_specs=[VMEM] * 3,
        out_specs=VMEM,
        scratch_shapes=[pltpu.VMEM(square, BF16)] * 4 + [DMA((4,))],
        compiler_params=pltpu.CompilerParams(
            collective_id=2, has_side_effects=True, vmem_limit_bytes=VMEM_BYTES
        ),
        name="adjoint_relay",
    )(residual, pair, aside)


def gated_kernel(
    state_ref, before_ref, local_ref, reach_ref, proj_ref, gain_ref, gated_ref, starts_ref, out_ref
):
    heads, groups = before_ref.shape[:2]
    block = proj_ref.shape[1] // heads

    @pl.loop(0, groups)
    def _(group):
        rows = pl.ds(pl.multiple_of(group * GROUP, GROUP), GROUP)
        shifted = pl.ds(pl.multiple_of(group * GROUP + RIM, RIM), GROUP)
        for head in range(heads):
            before = before_ref[head, group]
            start = dot_mid(before[:, :WIDTH], state_ref[head]) + before[:, WIDTH:]
            starts_ref[head, group] = start
            out = local_ref[head, group] + dot_mid(reach_ref[head, group], start)
            span = slice(head * WIDTH, (head + 1) * WIDTH)
            out_ref[rows, span] = out
            scale = lax.rsqrt(row_sum(out * out) / WIDTH + EPSILON)
            gate = proj_ref[shifted, (head + 1) * block - WIDTH : (head + 1) * block]
            gated = out * scale * gain_ref[:, span] * (gate * jax.nn.sigmoid(gate))
            gated_ref[rows, span] = gated.astype(BF16)


def gated_output(state, before, local, reach, proj, gain, rows_here):
    heads, groups = before.shape[:2]
    return pl.pallas_call(
        gated_kernel,
        out_shape=[
            shape((rows_here, heads * WIDTH), BF16),
            shape((heads, groups, WIDTH, WIDTH), F32),
            shape((rows_here, heads * WIDTH), F32),
        ],
        in_specs=[VMEM] * 6,
        out_specs=[VMEM] * 3,
        compiler_params=pltpu.CompilerParams(vmem_limit_bytes=VMEM_BYTES),
        name="mixer_output",
    )(state, before, local, reach, proj, gain)


def gather_rows_kernel(source, rows, sends, receives, local):
    greet(head_neighbours())
    span = source.shape[1]
    gather = HeadGather(
        source,
        lambda origin: rows.at[:, pl.ds(pl.multiple_of(origin * span, span), span)],
        sends,
        receives,
    )
    gather.start(local)
    gather.hand_on()
    gather.finish()


def gather_rows(values, n_head):
    return pl.pallas_call(
        gather_rows_kernel,
        out_shape=shape((values.shape[0], values.shape[1] * n_head), values.dtype),
        in_specs=[ANY],
        out_specs=ANY,
        scratch_shapes=[DMA((n_head, n_head // 2)), DMA((n_head,)), DMA],
        compiler_params=pltpu.CompilerParams(
            collective_id=3, has_side_effects=True, vmem_limit_bytes=VMEM_BYTES
        ),
        name="gather_gated",
    )(values)


def forward_kernel(
    rows_ref,
    gated_ref,
    w_out_ref,
    gain_ref,
    gate_ref,
    up_ref,
    down_ref,
    grad_ref,
    hidden_ref,
    normed_ref,
    inner_ref,
    out_ref,
    grad_gate_ref,
    grad_up_ref,
    grad_normed_ref,
):
    rows_here, model = rows_ref.shape
    heads, _, span = w_out_ref.shape
    tile = min(256, rows_here)

    @pl.loop(0, rows_here // tile)
    def _(at):
        rows = pl.ds(pl.multiple_of(at * tile, tile), tile)
        hidden = rows_ref[rows, :].astype(F32)
        for head in range(heads):
            part = gated_ref[rows, head * span : (head + 1) * span]
            hidden = hidden + dot(part, w_out_ref[head], (1, 1))
        hidden_ref[rows, :] = hidden
        scale = lax.rsqrt(row_sum(hidden * hidden) / model + EPSILON)
        normed = (hidden * scale * gain_ref[...]).astype(BF16)
        normed_ref[rows, :] = normed
        gate = dot(normed, gate_ref[...])
        up = dot(normed, up_ref[...])
        sigma = jax.nn.sigmoid(gate)
        swish = gate * sigma
        inner = (swish * up).astype(BF16)
        inner_ref[rows, :] = inner
        out_ref[rows, :] = dot(inner, down_ref[...], (1, 1)).astype(BF16)
        grad_inner = dot(grad_ref[rows, :], down_ref[...])
        grad_gate = (grad_inner * up * sigma * (1.0 + gate * (1.0 - sigma))).astype(BF16)
        grad_up = (grad_inner * swish).astype(BF16)
        grad_gate_ref[rows, :] = grad_gate
        grad_up_ref[rows, :] = grad_up
        back = dot(grad_gate, gate_ref[...], (1, 1)) + dot(grad_up, up_ref[...], (1, 1))
        grad_normed_ref[rows, :] = back.astype(BF16)


def feed_forward(rows, gated, w_out, gain, gate_in, up_in, down, grad_rows):
    rows_here, model = rows.shape
    units = gate_in.shape[1]
    return pl.pallas_call(
        forward_kernel,
        out_shape=[
            shape((rows_here, model), F32),
            shape((rows_here, model), BF16),
            shape((rows_here, units), BF16),
            shape((rows_here, model), BF16),
            shape((rows_here, units), BF16),
            shape((rows_here, units), BF16),
            shape((rows_here, model), BF16),
        ],
        in_specs=[VMEM] * 8,
        out_specs=[VMEM] * 7,
        compiler_params=pltpu.CompilerParams(vmem_limit_bytes=VMEM_BYTES),
        name="feed_forward",
    )(rows, gated, w_out, gain, gate_in, up_in, down, grad_rows)


class HeadSum:
    def __init__(self, source, cores, chips, sends, receives):
        self.source, self.cores, self.chips = source, cores, chips
        self.sends, self.receives = sends, receives
        self.span = source.shape[1] // lax.axis_size("head")

    def links(self):
        me_seq, me_head = lax.axis_index("seq"), lax.axis_index("head")
        return me_seq, me_head, lax.axis_size("head") // 2

    def columns(self, origin):
        return pl.ds(pl.multiple_of(origin * self.span, self.span), self.span)

    def to_core(self, at):
        me_seq, me_head, outer = self.links()
        far = 2 * at + 1 - lax.rem(me_head, 2)
        return remote(
            self.source.at[:, self.columns(far)],
            self.cores.at[at],
            self.sends.at[at],
            self.receives.at[at],
            (me_seq, other_of(me_head)),
        )

    def start(self):
        for at in range(self.links()[2]):
            self.to_core(at).start()

    def add_core(self, at):
        me_seq, me_head, outer = self.links()
        self.to_core(at).wait()
        near = 2 * at + lax.rem(me_head, 2)
        tile = min(128, self.source.shape[0])

        @pl.loop(0, self.source.shape[0] // tile)
        def _(turn):
            rows = pl.ds(pl.multiple_of(turn * tile, tile), tile)
            total = self.source[rows, self.columns(near)].astype(F32) + self.cores[at, rows, :].astype(F32)
            self.cores[at, rows, :] = total.astype(BF16)


def norm_kernel(
    partial_ref,
    out_ref,
    hidden_ref,
    grad_ref,
    gain_ref,
    result_ref,
    grad_hidden_ref,
    branch_ref,
    grad_gain_ref,
    total,
    cores,
    chips,
    out_cores,
    out_chips,
    sends,
    receives,
    chip_sends,
    chip_receives,
    last_sends,
    last_receives,
):
    rows_here, model = partial_ref.shape
    me_seq, me_head = lax.axis_index("seq"), lax.axis_index("head")
    outer = lax.axis_size("head") // 2
    chip, core = me_head // 2, lax.rem(me_head, 2)
    span = model // (2 * outer)
    greet(head_neighbours())
    back = HeadSum(partial_ref, cores, chips, sends.at[0], receives.at[0])
    ahead = HeadSum(out_ref, out_cores, out_chips, sends.at[1], receives.at[1])
    back.start()
    ahead.start()

    def columns(origin):
        return pl.ds(pl.multiple_of(origin * span, span), span)

    def to_chip(step):
        return remote(
            cores,
            chips.at[step],
            chip_sends.at[0, step],
            chip_receives.at[0, step],
            (me_seq, lax.rem(me_head + 2 * step, 2 * outer)),
        )

    def out_to_chip(step):
        target = lax.rem(me_head + 2 * step, 2 * outer)
        return remote(
            out_cores.at[target // 2],
            out_chips.at[step],
            chip_sends.at[1, step],
            chip_receives.at[1, step],
            (me_seq, target),
        )

    for at in range(outer):
        back.add_core(at)
    for step in range(1, outer):
        to_chip(step).start()
    for at in range(outer):
        ahead.add_core(at)
    for step in range(1, outer):
        out_to_chip(step).start()
    for step in range(1, outer):
        to_chip(step).wait()
    tile = min(128, rows_here)

    def to_total(at):
        far = columns(2 * at + core)
        return remote(
            total.at[:, far],
            total.at[:, far],
            last_sends.at[at],
            last_receives.at[at],
            (me_seq, other_of(me_head)),
        )

    for at in range(outer):

        @pl.loop(0, rows_here // tile)
        def _(turn):
            rows = pl.ds(pl.multiple_of(turn * tile, tile), tile)
            value = cores[at, rows, :].astype(F32)
            for step in range(1, outer):
                value = value + chips[step, at, rows, :].astype(F32)
            total[rows, columns(2 * at + core)] = value.astype(BF16)

        to_total(at).start()
    for at in range(outer):
        to_total(at).wait()

    own = columns(me_head)
    grad_gain_ref[...] = jnp.zeros_like(grad_gain_ref)

    @pl.loop(0, rows_here // tile)
    def _(turn):
        rows = pl.ds(pl.multiple_of(turn * tile, tile), tile)
        hidden = hidden_ref[rows, :]
        scale = lax.rsqrt(row_sum(hidden * hidden) / model + EPSILON)
        weighted = total[rows, :].astype(F32) * gain_ref[...]
        inner = row_sum(weighted * hidden)
        grad = scale * weighted - hidden * (scale * scale * scale * inner / model)
        grad = grad + grad_ref[rows, :].astype(F32)
        branch_ref[rows, :] = grad.astype(BF16)

    @pl.loop(0, rows_here // tile)
    def _(turn):
        rows = pl.ds(pl.multiple_of(turn * tile, tile), tile)
        whole = hidden_ref[rows, :]
        scale = lax.rsqrt(row_sum(whole * whole) / model + EPSILON)
        weighted = total[rows, :].astype(F32) * gain_ref[...]
        inner = row_sum(weighted * whole)
        hidden = hidden_ref[rows, own]
        back_rows = total[rows, own].astype(F32)
        grad = scale * back_rows * gain_ref[:, own] - hidden * (scale * scale * scale * inner / model)
        grad_hidden_ref[rows, :] = grad + grad_ref[rows, own].astype(F32)
        grad_gain_ref[...] += jnp.sum(back_rows * hidden * scale, axis=0, keepdims=True)

    for step in range(1, outer):
        out_to_chip(step).wait()

    @pl.loop(0, rows_here // tile)
    def _(turn):
        rows = pl.ds(pl.multiple_of(turn * tile, tile), tile)
        value = hidden_ref[rows, own] + out_cores[chip, rows, :].astype(F32)
        for step in range(1, outer):
            value = value + out_chips[step, rows, :].astype(F32)
        result_ref[rows, :] = value.astype(BF16)


def norm_back(partial_sum, out, hidden, grad_rows, gain, n_head):
    rows_here, model = hidden.shape
    span, outer = model // n_head, n_head // 2
    return pl.pallas_call(
        norm_kernel,
        out_shape=[
            shape((rows_here, span), BF16),
            shape((rows_here, span), F32),
            shape((rows_here, model), BF16),
            shape((1, span), F32),
        ],
        in_specs=[VMEM] * 5,
        out_specs=[VMEM] * 4,
        scratch_shapes=[
            pltpu.VMEM((rows_here, model), BF16),
            pltpu.VMEM((outer, rows_here, span), BF16),
            pltpu.VMEM((outer, outer, rows_here, span), BF16),
            pltpu.VMEM((outer, rows_here, span), BF16),
            pltpu.VMEM((outer, rows_here, span), BF16),
            DMA((2, outer)),
            DMA((2, outer)),
            DMA((2, outer)),
            DMA((2, outer)),
            DMA((outer,)),
            DMA((outer,)),
        ],
        compiler_params=pltpu.CompilerParams(
            collective_id=4, has_side_effects=True, vmem_limit_bytes=VMEM_BYTES
        ),
        name="second_norm_back",
    )(partial_sum, out, hidden, grad_rows, gain)


def gate_back_kernel(
    branch_ref,
    w_out_ref,
    out_ref,
    proj_ref,
    gain_ref,
    reach_ref,
    map_ref,
    grad_out_ref,
    grad_gate_ref,
    grad_gain_ref,
    residual_ref,
    total_ref,
):
    heads, groups = reach_ref.shape[:2]
    block = proj_ref.shape[1] // heads
    grad_gain_ref[...] = jnp.zeros_like(grad_gain_ref)
    for head in range(heads):
        total_ref[head] = jnp.zeros((WIDTH, WIDTH), F32)

    @pl.loop(0, groups)
    def _(turn):
        group = groups - 1 - turn
        rows = pl.ds(pl.multiple_of(group * GROUP, GROUP), GROUP)
        shifted = pl.ds(pl.multiple_of(group * GROUP + RIM, RIM), GROUP)
        grad_gated = dot(branch_ref[rows, :], w_out_ref[...])
        for head in range(heads):
            span = slice(head * WIDTH, (head + 1) * WIDTH)
            gain = gain_ref[:, span]
            out = out_ref[rows, span]
            scale = lax.rsqrt(row_sum(out * out) / WIDTH + EPSILON)
            gate = proj_ref[shifted, (head + 1) * block - WIDTH : (head + 1) * block]
            sigma = jax.nn.sigmoid(gate)
            grad = grad_gated[:, span]
            scaled = out * scale
            grad_normed = grad * gate * sigma
            grad_gate_ref[rows, span] = (
                grad * scaled * gain * sigma * (1.0 + gate * (1.0 - sigma))
            ).astype(BF16)
            grad_gain_ref[:, span] += jnp.sum(grad_normed * scaled, axis=0, keepdims=True)
            weighted = grad_normed * gain
            grad_out = scale * (weighted - scaled * (row_sum(weighted * scaled) / WIDTH))
            grad_out_ref[rows, span] = grad_out
            residual = dot_mid(reach_ref[head, group], grad_out, (0, 0))
            residual_ref[head, group] = residual
            total_ref[head] = residual + dot_mid(map_ref[head, group], total_ref[head], (0, 0))


def gate_back(branch, w_out, out, proj, gain, reach, maps):
    heads, groups = reach.shape[:2]
    rows_here = branch.shape[0]
    return pl.pallas_call(
        gate_back_kernel,
        out_shape=[
            shape((rows_here, heads * WIDTH), F32),
            shape((rows_here, heads * WIDTH), BF16),
            shape((1, heads * WIDTH), F32),
            shape((heads, groups, WIDTH, WIDTH), F32),
            shape((heads, WIDTH, WIDTH), F32),
        ],
        in_specs=[VMEM] * 7,
        out_specs=[VMEM] * 5,
        compiler_params=pltpu.CompilerParams(vmem_limit_bytes=VMEM_BYTES),
        name="mixer_gate_back",
    )(branch, w_out, out, proj, gain, reach, maps)


def mixer_back_kernel(
    lengths_ref,
    rate_ref,
    adjoint_ref,
    proj_ref,
    small_ref,
    taps_ref,
    query_ref,
    key_ref,
    value_ref,
    inverse_ref,
    solved_ref,
    lower_ref,
    scores_ref,
    starts_ref,
    map_ref,
    grad_out_ref,
    residual_ref,
    grad_proj_ref,
    grad_small_ref,
    grad_taps_ref,
    grad_rate_ref,
    running,
):
    heads, groups = key_ref.shape[:2]
    block = proj_ref.shape[1] // heads
    channels = (1 + 2 * HOUSE) * WIDTH
    rows_here = groups * GROUP
    first = lax.axis_index("seq") * rows_here
    bounds = bounds_of(lengths_ref)
    grad_proj_ref[...] = jnp.zeros_like(grad_proj_ref)
    grad_taps_ref[...] = jnp.zeros_like(grad_taps_ref)
    grad_rate_ref[...] = jnp.zeros_like(grad_rate_ref)
    running[...] = adjoint_ref[...]

    @pl.loop(0, groups)
    def _(turn):
        group = groups - 1 - turn
        keeps = conv_keeps(group, first, bounds)
        masks = group_masks(group, first, bounds)
        rows = pl.ds(pl.multiple_of(group * GROUP, GROUP), GROUP)
        small_parts = []
        for head in range(heads):
            span = slice(head * WIDTH, (head + 1) * WIDTH)
            betas, decay_logit, soft, cumulative = gate_terms(
                small_ref, rate_ref[head], group, head
            )
            beta = jnp.concatenate([betas[:, 0:1], betas[:, 1:2]], axis=0)
            decay, growth, to_end = decay_terms(cumulative, masks)
            query, keys, values = query_ref[head, group], key_ref[head, group], value_ref[head, group]
            lower, scores = lower_ref[head, group], scores_ref[head, group]
            solved, start = solved_ref[head, group], starts_ref[head, group]
            grad_out = grad_out_ref[rows, span]
            after = running[head]
            running[head] = residual_ref[head, group] + dot_mid(map_ref[head, group], after, (0, 0))
            updates = solved[:, :WIDTH] - dot_mid(solved[:, WIDTH:], start)
            carried = to_end * keys
            grad_reach = dot_mid(grad_out, start, (1, 1))
            grad_scores = dot_mid(grad_out, updates, (1, 1))
            grad_updates = dot_mid(scores, grad_out, (0, 0)) + dot_mid(carried, after)
            grad_carried = dot_mid(updates, after, (1, 1))
            grad_total = jnp.sum(row_sum(start * after), axis=0, keepdims=True)
            grad_pull = -dot_mid(grad_updates, start, (1, 1))
            right = dot_mid(
                inverse_ref[head, group],
                jnp.concatenate([grad_updates, grad_pull], axis=1),
                (0, 0),
            )
            grad_lower = jnp.where(masks[1], -dot_mid(right, solved, (1, 1)), 0.0)
            right_value, right_key = right[:, :WIDTH], right[:, WIDTH:]
            grad_values = beta * right_value
            by_key = row_sum(right_key * keys)
            weighted = grad_lower * lower
            grad_beta = row_sum(right_value * values) + by_key * growth
            inner_decay = decay * dot_mid(keys, keys, (1, 1))
            grad_beta = grad_beta + row_sum(grad_lower * inner_decay)
            grad_growth = by_key * beta
            grad_inner = grad_lower * decay * beta
            pairs = grad_scores * decay[GROUP:]
            grad_query = growth[GROUP:] * grad_reach + dot_mid(pairs, keys)
            grad_keys = (
                (beta * growth) * right_key
                + to_end * grad_carried
                + dot_mid(pairs, query, (0, 0))
                + dot_mid(grad_inner, keys)
                + dot_mid(grad_inner, keys, (0, 0))
            )
            by_end = row_sum(grad_carried * keys) * to_end
            by_reach = row_sum(grad_reach * query)
            score_part = grad_scores * scores
            spread = weighted + jnp.concatenate([jnp.zeros_like(score_part), score_part], axis=0)
            is_last = rows_of(MICRO) == MICRO - 1
            grad_growth = grad_growth + jnp.concatenate([jnp.zeros_like(by_reach), by_reach], axis=0)
            grad_growth = grad_growth + jnp.where(is_last, grad_total, 0.0)
            column = row_sum(spread) - by_end + grad_growth * growth
            column = column + jnp.where(is_last, jnp.sum(by_end, axis=0, keepdims=True), 0.0)
            column = column - to_column(jnp.sum(spread, axis=0, keepdims=True))
            per_token = column[:GROUP] + column[GROUP:]
            later = lanes_of(GROUP) >= rows_of(GROUP)
            grad_log_decay = row_sum(jnp.where(later, to_lane(per_token), 0.0))
            rate = rate_ref[head]
            grad_rate_ref[0:1, head : head + 1] += jnp.sum(
                -grad_log_decay * soft, axis=0, keepdims=True
            )
            grad_logit = -rate * grad_log_decay * jax.nn.sigmoid(decay_logit)
            grad_beta = grad_beta * beta * (1.0 - 0.5 * beta)
            small_parts += [grad_beta[:GROUP], grad_beta[GROUP:], grad_logit]
            grads = [
                grad_query,
                grad_keys[:GROUP],
                grad_keys[GROUP:],
                grad_values[:GROUP],
                grad_values[GROUP:],
            ]
            units = [query, keys[:GROUP], keys[GROUP:]]
            for part, grad in enumerate(grads):
                column_at = head * block + part * WIDTH
                taps_at = head * channels + part * WIDTH
                parts = conv_window(proj_ref, group, column_at)
                total = conv_total(parts, keeps, taps_ref, taps_at)
                sigma = jax.nn.sigmoid(total)
                if part < 1 + HOUSE:
                    mixed = total * sigma
                    scale = lax.rsqrt(row_sum(mixed * mixed) + EPSILON)
                    unit = units[part]
                    grad = scale * (grad - unit * row_sum(grad * unit))
                grad = grad * sigma * (1.0 + total * (1.0 - sigma))
                taps_span = slice(taps_at, taps_at + WIDTH)
                window = jnp.zeros((GROUP + 8, WIDTH), F32)
                for step in range(4):
                    kept = grad if step == 0 else grad * keeps[step]
                    grad_taps_ref[step : step + 1, taps_span] += jnp.sum(
                        kept * parts[step], axis=0, keepdims=True
                    )
                    moved = kept * taps_ref[step : step + 1, taps_span]
                    pieces = [jnp.zeros((8 - step, WIDTH), F32), moved]
                    if step:
                        pieces.append(jnp.zeros((step, WIDTH), F32))
                    window = window + jnp.concatenate(pieces, axis=0)
                place = pl.ds(pl.multiple_of(group * GROUP + RIM - 8, 8), GROUP + 8)
                grad_proj_ref[place, taps_span] += window
        padding = jnp.zeros((GROUP, WIDTH - len(small_parts)), F32)
        grad_small_ref[rows, :] = jnp.concatenate(small_parts + [padding], axis=1).astype(BF16)


def mixer_back(
    lengths,
    rate,
    adjoint,
    proj,
    small,
    taps,
    query,
    keys,
    values,
    inverse,
    solved,
    lower,
    scores,
    starts,
    maps,
    grad_out,
    residual,
):
    heads, groups = keys.shape[:2]
    rows_here = groups * GROUP
    channels = taps.shape[1]
    return pl.pallas_call(
        mixer_back_kernel,
        out_shape=[
            shape((rows_here + RIM, channels), F32),
            shape((rows_here, WIDTH), BF16),
            shape((8, channels), F32),
            shape((8, WIDTH), F32),
        ],
        in_specs=[SMEM, SMEM] + [VMEM] * 15,
        out_specs=[VMEM] * 4,
        scratch_shapes=[pltpu.VMEM((heads, WIDTH, WIDTH), F32)],
        compiler_params=pltpu.CompilerParams(vmem_limit_bytes=VMEM_BYTES),
        name="mixer_back",
    )(
        lengths,
        rate,
        adjoint,
        proj,
        small,
        taps,
        query,
        keys,
        values,
        inverse,
        solved,
        lower,
        scores,
        starts,
        maps,
        grad_out,
        residual,
    )


def spread_kernel(count, *refs):
    refs = list(refs)
    take = lambda number: [refs.pop(0) for _ in range(number)]
    partials, outs, sides, ups, downs = (take(count) for _ in range(5))
    side_sends, side_receives, way_sends, way_receives = take(4)
    me_seq, me_head, outer, place, inner = seq_links()
    greet(seq_neighbours())

    def to_side(at, far):
        return remote(
            partials[at].at[2 * far + 1 - inner],
            sides[at].at[far],
            side_sends.at[at, far],
            side_receives.at[at, far],
            (other_of(me_seq), me_head),
        )

    def up(at, far):
        return remote(
            sides[at].at[far],
            ups[at].at[far],
            way_sends.at[0, at, far],
            way_receives.at[0, at, far],
            (me_seq + 2, me_head),
        )

    def down(at, far):
        return remote(
            sides[at].at[far],
            downs[at].at[far],
            way_sends.at[1, at, far],
            way_receives.at[1, at, far],
            (me_seq - 2, me_head),
        )

    def add(at, far, terms, target):
        depth = partials[at].shape[1]
        tile = min(depth, 64)

        @pl.loop(0, depth // tile)
        def _(turn):
            rows = pl.ds(pl.multiple_of(turn * tile, tile), tile)
            total = terms[0](rows).astype(F32)
            for term in terms[1:]:
                total = total + term(rows).astype(F32)
            target(rows, total)

    order = sorted(range(outer), key=lambda far: -abs(2 * far + 1 - outer))
    for far in order:
        for at in range(count):
            to_side(at, far).start()
    for far in order:
        for at in range(count):
            to_side(at, far).wait_recv()

            def keep(rows, total, at=at, far=far):
                sides[at][far, rows, :] = total.astype(sides[at].dtype)

            mine = lambda rows, at=at, far=far: partials[at][2 * far + inner, rows, :]
            side = lambda rows, at=at, far=far: sides[at][far, rows, :]
            add(at, far, [mine, side], keep)

            @pl.when(far > place)
            def _():
                @pl.when(place > 0)
                def _():
                    up(at, far).wait_recv()
                    below = lambda rows, at=at, far=far: ups[at][far, rows, :]
                    add(at, far, [side, below], keep)

                up(at, far).start()

            @pl.when(far < place)
            def _():
                @pl.when(place < outer - 1)
                def _():
                    down(at, far).wait_recv()
                    above = lambda rows, at=at, far=far: downs[at][far, rows, :]
                    add(at, far, [side, above], keep)

                down(at, far).start()

    for at in range(count):

        def store(rows, total, at=at):
            outs[at][rows, :] = total

        side = lambda rows, at=at: sides[at][place, rows, :]
        below = lambda rows, at=at: ups[at][place, rows, :]
        above = lambda rows, at=at: downs[at][place, rows, :]

        @pl.when(place > 0)
        def _():
            up(at, place).wait_recv()

        @pl.when(place < outer - 1)
        def _():
            down(at, place).wait_recv()

        @pl.when(place == 0)
        def _():
            add(at, place, [side, above], store)

        @pl.when(place == outer - 1)
        def _():
            add(at, place, [side, below], store)

        @pl.when((place > 0) & (place < outer - 1))
        def _():
            add(at, place, [side, below, above], store)

    for at in range(count):
        for far in range(outer):
            to_side(at, far).wait_send()

            @pl.when(far > place)
            def _():
                up(at, far).wait_send()

            @pl.when(far < place)
            def _():
                down(at, far).wait_send()


def spread_sums(partials):
    count = len(partials)
    n_seq = partials[0].shape[0]
    outer = n_seq // 2
    buffers = [pltpu.VMEM((outer,) + a.shape[1:], a.dtype) for a in partials]
    return pl.pallas_call(
        partial(spread_kernel, count),
        out_shape=[shape(a.shape[1:], F32) for a in partials],
        in_specs=[VMEM] * count,
        out_specs=[VMEM] * count,
        scratch_shapes=buffers * 3
        + [
            DMA((count, outer)),
            DMA((count, outer)),
            DMA((2, count, outer)),
            DMA((2, count, outer)),
        ],
        compiler_params=pltpu.CompilerParams(
            collective_id=5, has_side_effects=True, vmem_limit_bytes=VMEM_BYTES
        ),
        name="sums_over_seq",
    )(*partials)


def entry_back_kernel(
    partial_ref,
    inner_ref,
    columns_ref,
    rows_ref,
    gain_ref,
    grad_hidden_ref,
    grad_ref,
    grad_gain_ref,
    cores,
    chips,
    inner_core,
    inner_chips,
    sends,
    receives,
    chip_sends,
    chip_receives,
):
    rows_here, model = partial_ref.shape
    me_seq, me_head = lax.axis_index("seq"), lax.axis_index("head")
    outer = lax.axis_size("head") // 2
    chip = me_head // 2
    greet(head_neighbours())
    back = HeadSum(partial_ref, cores, chips, sends, receives)
    back.start()

    def inner_to_core():
        return remote(
            inner_ref,
            inner_core,
            sends.at[outer],
            receives.at[outer],
            (me_seq, other_of(me_head)),
        )

    def to_chip(step):
        target = lax.rem(me_head + 2 * step, 2 * outer)
        return remote(
            cores.at[target // 2],
            chips.at[step],
            chip_sends.at[0, step],
            chip_receives.at[0, step],
            (me_seq, target),
        )

    def inner_to_chip(step):
        return remote(
            inner_core,
            inner_chips.at[step],
            chip_sends.at[1, step],
            chip_receives.at[1, step],
            (me_seq, lax.rem(me_head + 2 * step, 2 * outer)),
        )

    inner_to_core().start()
    for at in range(outer):
        back.add_core(at)
    inner_to_core().wait()
    inner_core[...] = inner_core[...] + inner_ref[...]
    for step in range(1, outer):
        inner_to_chip(step).start()
        to_chip(step).start()
    for step in range(1, outer):
        inner_to_chip(step).wait()
        to_chip(step).wait()
    inner_total = inner_core[...]
    for step in range(1, outer):
        inner_total = inner_total + inner_chips[step]
    inner_core[...] = inner_total
    span = model // (2 * outer)
    own = pl.ds(pl.multiple_of(me_head * span, span), span)
    grad_gain_ref[...] = jnp.zeros_like(grad_gain_ref)
    tile = 128

    @pl.loop(0, rows_here // tile)
    def _(turn):
        rows = pl.ds(pl.multiple_of(turn * tile, tile), tile)
        whole = rows_ref[rows, :].astype(F32)
        scale = lax.rsqrt(row_sum(whole * whole) / model + EPSILON)
        inner = to_column(inner_core[pl.ds(turn, 1), :])
        total = cores[chip, rows, :].astype(F32)
        for step in range(1, outer):
            total = total + chips[step, rows, :].astype(F32)
        values = columns_ref[rows, :].astype(F32)
        grad = scale * total * gain_ref[:, own] - values * (scale * scale * scale * inner / model)
        grad_ref[rows, :] = grad + grad_hidden_ref[rows, :]
        grad_gain_ref[...] += jnp.sum(total * values * scale, axis=0, keepdims=True)


def entry_back(partial_sum, inner, columns, rows, gain, grad_hidden, n_head):
    rows_here, model = rows.shape
    span, outer = model // n_head, n_head // 2
    return pl.pallas_call(
        entry_back_kernel,
        out_shape=[shape((rows_here, span), F32), shape((1, span), F32)],
        in_specs=[VMEM] * 6,
        out_specs=[VMEM] * 2,
        scratch_shapes=[
            pltpu.VMEM((outer, rows_here, span), BF16),
            pltpu.VMEM((outer, rows_here, span), BF16),
            pltpu.VMEM(inner.shape, F32),
            pltpu.VMEM((outer,) + inner.shape, F32),
            DMA((outer + 1,)),
            DMA((outer + 1,)),
            DMA((2, outer)),
            DMA((2, outer)),
        ],
        compiler_params=pltpu.CompilerParams(
            collective_id=6, has_side_effects=True, vmem_limit_bytes=VMEM_BYTES
        ),
        name="first_norm_back",
    )(partial_sum, inner, columns, rows, gain, grad_hidden)


def tiled(flat, rows):
    return jnp.pad(flat, (0, rows * WIDTH - flat.shape[0])).reshape(rows, WIDTH)


def on_device(
    n_seq,
    n_head,
    inputs,
    lengths,
    norm1_gain,
    w_in,
    w_small,
    conv_weight,
    decay_rate,
    out_gain,
    w_out,
    norm2_gain,
    w_gate,
    w_up,
    w_down,
    cotangent,
):
    rows_here, span = inputs.shape
    model = span * n_head
    heads = decay_rate.shape[0]
    small_count = w_small.shape[1]
    me_head = lax.axis_index("head")

    pieces = [norm1_gain, norm2_gain, out_gain, conv_weight.reshape(-1), w_small.reshape(-1)]
    sizes = [piece.shape[0] for piece in pieces]
    tile_rows = -(-sum(sizes) // (16 * WIDTH)) * 16
    tile = tiled(jnp.concatenate(pieces), tile_rows)
    shards = [tile, w_out.T, w_in, w_gate, w_up, w_down.T]
    rows, grad_rows, rim, gathered, wide = entry(inputs, cotangent, shards, 2, n_seq, n_head)
    flat = wide[0].reshape(n_head, n_seq, -1)
    cuts = [0]
    for size in sizes:
        cuts.append(cuts[-1] + size)
    piece_of = lambda at: flat[:, :, cuts[at] : cuts[at + 1]]
    gain_one = piece_of(0).reshape(1, model).astype(F32)
    gain_two = piece_of(1).reshape(1, model).astype(F32)
    mine = lax.dynamic_index_in_dim(flat, me_head, 0, keepdims=False)
    own_of = lambda at: mine[:, cuts[at] : cuts[at + 1]]
    gain_heads = own_of(2).reshape(1, heads * WIDTH).astype(F32)
    taps = jnp.swapaxes(own_of(3).reshape(n_seq, 4, -1), 0, 1).reshape(4, -1).astype(F32)
    proj_small = jnp.pad(own_of(4).reshape(model, small_count), ((0, 0), (0, WIDTH - small_count)))
    w_out_all = wide[1].reshape(n_head, model, -1)
    w_out_own = gathered[1].reshape(model, -1)
    proj_in = gathered[2].reshape(model, -1)
    gate_in = gathered[3].reshape(model, -1)
    up_in = gathered[4].reshape(model, -1)
    down = gathered[5].reshape(model, -1)

    (
        normed_one,
        proj,
        small,
        query,
        keys,
        values,
        inverse,
        solved,
        lower,
        scores,
        reach,
        local,
        maps,
        adds,
        before,
        total,
    ) = mixer(lengths, decay_rate, rows, rim, gain_one, proj_in, proj_small, taps)
    state, pair, aside = carry_state(total)
    gated, starts, out = gated_output(state, before, local, reach, proj, gain_heads, rows_here)
    gated_rows = gather_rows(gated, n_head)
    hidden, normed_two, inner, out_part, grad_gate, grad_up, back_part = feed_forward(
        rows, gated_rows, w_out_all, gain_two, gate_in, up_in, down, grad_rows
    )
    result, grad_hidden, branch, grad_gain_two = norm_back(
        back_part, out_part, hidden, grad_rows, gain_two, n_head
    )
    grad_mixed, grad_gate_part, grad_gain_heads, residual, residual_total = gate_back(
        branch, w_out_own, out, proj, gain_heads, reach, maps
    )
    own_map = total[:, :, :WIDTH].astype(BF16).astype(F32)
    adjoint = carry_adjoint(
        residual_total, jnp.concatenate([pair[:, :, :WIDTH], own_map], axis=2), aside
    )
    grad_conv, grad_small, grad_taps, grad_rate = mixer_back(
        lengths,
        decay_rate,
        adjoint,
        proj,
        small,
        taps,
        query,
        keys,
        values,
        inverse,
        solved,
        lower,
        scores,
        starts,
        maps,
        grad_mixed,
        residual,
    )
    back_links = [(source, source - 1) for source in range(1, n_seq)]
    returned = lax.ppermute(grad_conv[RIM - 3 : RIM], "seq", back_links)
    grad_conv = grad_conv[RIM:].at[rows_here - 3 :].add(returned)
    grad_projected = jnp.concatenate(
        [
            grad_conv.reshape(rows_here, heads, -1).astype(BF16),
            grad_gate_part.reshape(rows_here, heads, -1),
        ],
        axis=2,
    ).reshape(rows_here, -1)
    grad_proj_in = jnp.dot(normed_one[RIM:].T, grad_projected, preferred_element_type=F32)
    grad_proj_small = jnp.dot(normed_one[RIM:].T, grad_small, preferred_element_type=F32)
    back_one = jnp.dot(grad_projected, proj_in.T, preferred_element_type=F32) + jnp.dot(
        grad_small, proj_small.T, preferred_element_type=F32
    )
    inner_one = jnp.sum(back_one * gain_one * rows.astype(F32), axis=1).reshape(-1, WIDTH)
    grad_inputs, grad_gain_one = entry_back(
        back_one.astype(BF16), inner_one, inputs, rows, gain_one, grad_hidden, n_head
    )
    grad_down = jnp.dot(grad_rows.T, inner, preferred_element_type=F32)
    grad_gate_in = jnp.dot(normed_two.T, grad_gate, preferred_element_type=F32)
    grad_up_in = jnp.dot(normed_two.T, grad_up, preferred_element_type=F32)
    grad_out = jnp.dot(branch.T, gated, preferred_element_type=F32)
    stacked = lambda values: values.astype(BF16).reshape(n_seq, -1, values.shape[1])
    taps_out = jnp.swapaxes(grad_taps[:4].reshape(4, n_seq, -1), 0, 1).reshape(n_seq, -1)
    rates = jnp.broadcast_to(grad_rate[0:1, :heads], (n_seq, heads))
    tail = jnp.concatenate(
        [
            grad_gain_one.reshape(n_seq, -1),
            grad_gain_two.reshape(n_seq, -1),
            grad_gain_heads.reshape(n_seq, -1),
            taps_out,
            grad_proj_small[:, :small_count].reshape(n_seq, -1),
            rates,
        ],
        axis=1,
    )
    tail_rows = -(-tail.shape[1] // (8 * WIDTH)) * 8
    tail = jnp.pad(tail, ((0, 0), (0, tail_rows * WIDTH - tail.shape[1])))
    sums = spread_sums(
        [
            stacked(grad_gate_in),
            stacked(grad_up_in),
            stacked(grad_down),
            stacked(grad_out),
            stacked(grad_proj_in),
            tail.reshape(n_seq, tail_rows, WIDTH),
        ]
    )
    flat_out = sums[5].reshape(-1)
    cut = lambda at: flat_out[cuts[at] : cuts[at + 1]]
    return (
        result,
        grad_inputs,
        cut(0),
        sums[4],
        cut(4).reshape(-1, small_count),
        cut(3).reshape(4, -1),
        flat_out[cuts[5] : cuts[5] + heads],
        cut(2),
        sums[3].T,
        cut(1),
        sums[0],
        sums[1],
        sums[2].T,
    )


def solution(mesh):
    return jax.shard_map(
        partial(on_device, mesh.shape["seq"], mesh.shape["head"]),
        mesh=mesh,
        in_specs=(
            P("seq", "head"),
            P(),
            P(("head", "seq")),
            P("seq", "head"),
            P("seq", "head"),
            P(None, ("head", "seq")),
            P("head"),
            P(("head", "seq")),
            P("head", "seq"),
            P(("head", "seq")),
            P("seq", "head"),
            P("seq", "head"),
            P("head", "seq"),
            P("seq", "head"),
        ),
        out_specs=(
            P("seq", "head"),
            P("seq", "head"),
            P(("head", "seq")),
            P("seq", "head"),
            P("seq", "head"),
            P(None, ("head", "seq")),
            P("head"),
            P(("head", "seq")),
            P("head", "seq"),
            P(("head", "seq")),
            P("seq", "head"),
            P("seq", "head"),
            P("head", "seq"),
        ),
        check_vma=False,
    )
```

time: 1430 us -> 491 us (0.34)
  the two profiles are of different devices: /device:TPU:0 before, /device:TPU:18 now
where the time goes in v1:
time: 491 us; the launch traced here: 490 us
  Pallas kernels  416 us (85%)
  local copies, waits for them, and re-layouts  49 us (10%)
  matrix products  15.1 us (3%)
  other arithmetic  6.83 us (1%)
    pallas_call x1, Pallas kernels, spread_sums(): pl.pallas_call(partial(spread_kernel, count), out_shape=[shape(a.shape[1:...  124 us
    pallas_call x1, Pallas kernels, entry(): pl.pallas_call(partial(entry_kernel, count, wide_count), out_shape=[shape...  114 us
    pallas_call x1, Pallas kernels, mixer(): pl.pallas_call(mixer_kernel, out_shape=[shape((rows_here + RIM, model), B...  33.4 us
    pallas_call x1, Pallas kernels, mixer_back(): pl.pallas_call(mixer_back_kernel, out_shape=[shape((rows_here + RIM, chan...  31.6 us
    pallas_call x1, Pallas kernels, norm_back(): pl.pallas_call(norm_kernel, out_shape=[shape((rows_here, span), BF16), sh...  25.8 us
    unnamed x60, local copies, waits for them, and re-layouts  19.8 us
    pallas_call x1, Pallas kernels, carry_state(): pl.pallas_call(state_kernel, out_shape=[shape(square, F32), shape(both, F...  17.9 us
    pallas_call x1, Pallas kernels, entry_back(): pl.pallas_call(entry_back_kernel, out_shape=[shape((rows_here, span), F32...  13.9 us
  transfers between devices with their start and end apart: 1, of which 0 were waited for; matrix products, arithmetic and copies ran while one was open for 4% of the time, Pallas kernels for 0%

profile of v1, /device:TPU:18, one launch (start us, length us, event | category | flops | bytes accessed | tf_op | source)
XLA Modules:
  0.0 490.1 jit_solution(876356332841279037)
XLA Ops:
  2.4 2.1 concatenate.14
  5.1 1.6 copy.40
  6.6 1.7 copy.42.refs_5_
  8.4 1.7 copy.43.refs_6_
  10.1 1.7 copy.41
  11.8 114.1 %entry_gathers.1 = (bf16[512,1024]{1,0:T(8,128)(2,1)}, bf16[512,1024]{1,0:T(8,128)(2,1)}, bf16[16,1024]{1,0:T(8,128)(2,1)}, bf16[8,16,128]{2,1,0:T(8,128)(2,1)},...) custom-call(bf16[512,256]{1,0:T(8,128)(2,1)} %columns_ref.1, ...), custom_call_target="tpu_custom_call" | custom-call | tf_op jit(solution)/shard_map/entry_gathers/pallas_call | solution.py:447
  130.0 33.4 %mixer_terms.1 = (bf16[528,1024]{1,0:T(8,128)(2,1)}, f32[528,1536]{1,0:T(8,128)}, f32[512,128]{1,0:T(8,128)}, f32[2,8,64,128]{3,2,1,0:T(8,128)}, f32[2,8,128,128...) custom-call(s32[8]{0:T(128)} %lengths_ref.3, ...), custom_call_target="tpu_custom_call" | custom-call | tf_op jit(solution)/shard_map/mixer_terms/pallas_call | solution.py:592
  164.3 17.9 %state_relay.1 = (f32[2,128,128]{2,1,0:T(8,128)}, f32[2,128,256]{2,1,0:T(8,128)}, f32[2,128,256]{2,1,0:T(8,128)}) custom-call(f32[2,128,256]{2,1,0:T(8,128)} %get-tuple-element.88.total_ref), custom_call_target="tpu_custom_call" | custom-call | tf_op jit(solution)/shard_map/state_relay/pallas_call | solution.py:665
  184.5 7.8 %mixer_output.1 = (bf16[512,256]{1,0:T(8,128)(2,1)}, f32[2,8,128,128]{3,2,1,0:T(8,128)}, f32[512,256]{1,0:T(8,128)}) custom-call(f32[2,128,128]{2,1,0:T(8,128)} %get-tuple-element.89.state_ref, f32[2,8,128,256]{3,2,1,0:T(8,128)} %get-tuple-element.90.before_ref, f32[2,8,64,128]{3,2,1,0:T(8,128)} %get-tuple-element.91.local_ref, ...), custom_call_target="tpu_custom_call" | custom-call | tf_op jit(solution)/shard_map/mixer_output/pallas_call | solution.py:760
  192.3 10.7 %gather_gated.1.gated_ref = bf16[512,1024]{1,0:T(8,128)(2,1)} custom-call(bf16[512,256]{1,0:T(8,128)(2,1)} %get-tuple-element.94.source), custom_call_target="tpu_custom_call" | custom-call | tf_op jit(solution)/shard_map/gather_gated/pallas_call | solution.py:789
  203.7 13.7 %feed_forward.1 = (f32[512,1024]{1,0:T(8,128)}, bf16[512,1024]{1,0:T(8,128)(2,1)}, bf16[512,704]{1,0:T(8,128)(2,1)}, bf16[512,1024]{1,0:T(8,128)(2,1)}, bf16[512...) custom-call(bf16[512,1024]{1,0:T(8,128)(2,1)} %get-tuple-element.84.rows_ref, ...), custom_call_target="tpu_custom_call" | custom-call | tf_op jit(solution)/shard_map/feed_forward/pallas_call | solution.py:853
  217.4 25.8 %second_norm_back.1 = (bf16[512,256]{1,0:T(8,128)(2,1)}, f32[512,256]{1,0:T(8,128)}, bf16[512,1024]{1,0:T(8,128)(2,1)}, f32[1,256]{1,0:T(1,128)}) custom-call(bf16[512,1024]{1,0:T(8,128)(2,1)} %get-tuple-element.100.partial_ref, bf16[512,1024]{1,0:T(8,128)(2,1)} %get-tuple-element.101.out_ref, f32[512,1024]{1,0:T(8,128)} %get-tuple-element.102.hidden_ref, ...), custom_call_target="tpu_custom_call" | custom-call | tf_op jit(solution)/shard_map/second_norm_back/pallas_call | solution.py:1045
  243.2 9.6 %mixer_gate_back.1 = (f32[512,256]{1,0:T(8,128)}, bf16[512,256]{1,0:T(8,128)(2,1)}, f32[1,256]{1,0:T(1,128)}, f32[2,8,128,128]{3,2,1,0:T(8,128)}, f32[2,128,128]{2,1,0:T(8,128)}) custom-call(bf16[512,1024]{1,0:T(8,128)(2,1)} %get-tuple-element.104.branch_ref, bf16[1024,256]{1,0:T(8,128)(2,1)} %bitcast.61, f32[512,256]{1,0:T(8,128)} %get-tuple-element.106.out_ref, ...), custom_call_target="tpu_custom_call" | custom-call | tf_op jit(solution)/shard_map/mixer_gate_back/pallas_call | solution.py:1126
  252.7 13.7 %adjoint_relay.1.adjoint_ref = f32[2,128,128]{2,1,0:T(8,128)} custom-call(f32[2,128,128]{2,1,0:T(8,128)} %get-tuple-element.108.residual_ref, f32[2,128,256]{2,1,0:T(8,128)} %pad_maximum_fusion.1.pair_ref, f32[2,128,256]{2,1,0:T(8,128)} %get-tuple-element.110.aside_ref), custom_call_target="tpu_custom_call" | custom-call | tf_op jit(solution)/shard_map/adjoint_relay/pallas_call | solution.py:722
  266.4 31.6 %mixer_back.1 = (f32[528,1280]{1,0:T(8,128)}, bf16[512,128]{1,0:T(8,128)(2,1)}, f32[8,1280]{1,0:T(8,128)}, f32[8,128]{1,0:T(8,128)}) custom-call(s32[8]{0:T(128)} %lengths_ref.3, f32[2]{0:T(128)} %rate_ref.3, f32[2,128,128]{2,1,0:T(8,128)} %adjoint_relay.1.adjoint_ref, f32[528,1536]{1,0:T(8,128)} %get-tuple-element.93.proj_ref, ...), custom_call_target="tpu_custom_call" | custom-call | tf_op jit(solution)/shard_map/mixer_back/pallas_call | solution.py:1309
  298.1 1.5 slice.88
  299.6 2.1 collective-permute-start
  303.0 2.1 convolution_convert_fusion.1
  306.3 2.1 convolution_convert_fusion.2
  310.4 1.9 slice.86
  313.6 2.6 copy.47
  319.1 2.6 copy.46
  321.7 1.6 copy.45
  326.4 1.6 copy-done.2
  328.1 1.8 fusion.8
  329.9 3.5 convolution_convert_fusion
  333.4 2.1 multiply_reduce_fusion
  335.5 13.9 %first_norm_back.1 = (f32[512,256]{1,0:T(8,128)}, f32[1,256]{1,0:T(1,128)}) custom-call(bf16[512,1024]{1,0:T(8,128)(2,1)} %get-tuple-element.170.partial_ref, f32[4,128]{1,0:T(4,128)} %bitcast.72, bf16[512,256]{1,0:T(8,128)(2,1)} %columns_ref.1, bf16[512,1024]{1,0:T(8,128)(2,1)} %get-tuple-element.84.rows_ref, f32[1,1024]{1,0:T(1,128)} %reshape.224.gain_ref, ...), custom_call_target="tpu_custom_call" | custom-call | tf_op jit(solution)/shard_map/first_norm_back/pallas_call | solution.py:1583
  351.7 123.9 %sums_over_seq.1 = (f32[128,704]{1,0:T(8,128)}, f32[128,704]{1,0:T(8,128)}, f32[128,704]{1,0:T(8,128)}, f32[128,256]{1,0:T(8,128)}, f32[128,1536]{1,0:T(8,128)}, /*index=5*/f32[16,128]{1,0:T(8,128)}) custom-call(bf16[8,128,704]{2,1,0:T(8,128)(2,1)} %bitcast.48, bf16[8,128,704]{2,1,0:T(8,128)(2,1)} %bitcast.47, bf16[8,128,704]{2,1,0:T(8,128)(2,1)} %bitcast.46, ...), custom_call_target="tpu_custom_call" | custom-call | tf_op jit(solution)/shard_map/sums_over_seq/pallas_call | solution.py:1472
  481.3 1.7 copy.51
  482.9 1.9 copy.52
  484.8 2.0 copy.53
  (103 shorter events, 33.1 us)
Async XLA Ops:
  266.4 35.3 %copy-start.3 = (bf16[512,1024]{1,0:T(8,128)(2,1)S(1)}, bf16[512,1024]{1,0:T(8,128)(2,1)}, u32[]{:S(2)}) copy-start(bf16[512,1024]{1,0:T(8,128)(2,1)} %get-tuple-element.104.branch_ref) | copy-start | bytes 3145732
  266.4 35.3 %copy-start.7 = (bf16[512,256]{1,0:T(8,128)(2,1)S(1)}, bf16[512,256]{1,0:T(8,128)(2,1)}, u32[]{:S(2)}) copy-start(bf16[512,256]{1,0:T(8,128)(2,1)} %get-tuple-element.94.source) | copy-start | bytes 786436
  298.0 5.0 %copy-start.1 = (bf16[512,1024]{1,0:T(8,128)(2,1)S(1)}, bf16[512,1024]{1,0:T(8,128)(2,1)}, u32[]{:S(2)}) copy-start(bf16[512,1024]{1,0:T(8,128)(2,1)} %get-tuple-element.99.grad_ref) | copy-start | bytes 3145732
  298.0 5.0 %copy-start.21 = (bf16[512,704]{1,0:T(8,128)(2,1)S(1)}, bf16[512,704]{1,0:T(8,128)(2,1)}, u32[]{:S(2)}) copy-start(bf16[512,704]{1,0:T(8,128)(2,1)} %get-tuple-element.130) | copy-start | bytes 2162692
  299.6 23.7 %collective-permute-start = (f32[3,1280]{1,0:T(4,128)}, f32[3,1280]{1,0:T(4,128)}, u32[]{:S(2)}, u32[]{:S(2)}) collective-permute-start(f32[3,1280]{1,0:T(4,128)} %slice.88), channel_id=1, source_target_pairs={{4,0},{8,4},{12,8},{16,12},{20,16},{24,20},{28,24},{5,1},{9,5},{13... | collective-permute-start | bytes 46088 | tf_op jit(solution)/shard_map/ppermute | solution.py:1712
  303.0 2.1 copy-start.18
  303.0 2.1 copy-start.20
  305.2 1.1 copy-start.19
  306.3 2.1 copy-start.10
  306.3 2.1 copy-start.16
  309.6 3.2 copy-start.14
  312.3 3.9 copy-start.13
  312.3 3.9 copy-start.15
  313.6 4.2 copy-start.9
  326.2 1.9 copy-start.2
  328.1 1.8 copy-start.17
  329.9 3.5 copy-start
  329.9 3.5 copy-start.11
  335.5 15.4 %copy-start.12 = (f32[8,640]{1,0:T(8,128)S(1)}, f32[8,640]{1,0:T(8,128)}, u32[]{:S(2)}) copy-start(f32[8,640]{1,0:T(8,128)} %reshape.218) | copy-start | bytes 61444
  475.5 11.3 %copy-start.6 = (f32[128,704]{1,0:T(8,128)S(1)}, f32[128,704]{1,0:T(8,128)}, u32[]{:S(2)}) copy-start(f32[128,704]{1,0:T(8,128)} %get-tuple-element.142) | copy-start | bytes 1081348
  475.5 12.2 %copy-start.8 = (bf16[512,256]{1,0:T(8,128)(2,1)S(1)}, bf16[512,256]{1,0:T(8,128)(2,1)}, u32[]{:S(2)}) copy-start(bf16[512,256]{1,0:T(8,128)(2,1)} %get-tuple-element.190) | copy-start | bytes 786436
  480.6 7.8 %copy-start.5 = (f32[512,256]{1,0:T(8,128)S(1)}, f32[512,256]{1,0:T(8,128)}, u32[]{:S(2)}) copy-start(f32[512,256]{1,0:T(8,128)} %get-tuple-element.191) | copy-start | bytes 1572868
  484.8 4.4 copy-start.4
